TPU v7x, 512 devices: a whole 4x8x8 slice. The times are simulated.
512 devices in a mesh: dp: 64 (over x, z, core), tensor: 8 (over y).
Axes of the slice: x: 4, y: 8, z: 8, core: 2. Of those that a mesh axis runs over, the one named last changes fastest.
Arguments:
- acts: bfloat16 [8192, 3072], P('dp', 'tensor'), may hold values from -6 to 6
- grads_out: bfloat16 [8192, 3072], P('dp', 'tensor'), may hold values from -1.5 to 1.5
- weight: bfloat16 [3072, 3072], P('dp', 'tensor'), may hold values from -0.109375 to 0.109375
- basis_init: float32 [64, 3072], P(None, 'tensor'), may hold values from -6 to 6
- feedback: bfloat16 [64, 3072, 3072], P('dp', None, 'tensor'), may hold values from -8 to 8
Outputs:
- input_grads: bfloat16 [8192, 3072], P('dp', 'tensor')
- new_feedback: bfloat16 [64, 3072, 3072], P('dp', None, 'tensor')
- update: float32 [3072, 3072], P('dp', 'tensor')
All inputs are finite; a program needn't handle non-finite values.
Results may differ from a plain program's by a relative error of at most 0.00055.
Values may be sent and summed in bfloat16 or wider, within the bound.
A program may use at most 64 MiB of HBM per device.

v0:
```python
import jax
import jax.numpy as jnp
from jax import lax
from jax.sharding import PartitionSpec as P


def local(acts, grads_out, weight, basis_init, feedback):
    highest = lax.Precision.HIGHEST
    gradient = lax.dot_general(
        lax.all_gather(acts, "tensor", axis=1, tiled=True),
        grads_out,
        (((0,), (0,)), ((), ())),
        preferred_element_type=jnp.float32,
    )
    partial_inputs = lax.dot_general(
        grads_out,
        lax.all_gather(weight, "dp", axis=0, tiled=True),
        (((1,), (1,)), ((), ())),
        preferred_element_type=jnp.float32,
    )
    feature_width = acts.shape[1]
    summed_inputs = lax.psum(partial_inputs, "tensor")
    input_grads = lax.dynamic_slice_in_dim(
        summed_inputs, lax.axis_index("tensor") * feature_width, feature_width, 1
    ).astype(jnp.bfloat16)
    total_grad = gradient + feedback[0].astype(jnp.float32)
    factor = lax.dot_general(
        basis_init,
        total_grad,
        (((1,), (1,)), ((), ())),
        precision=highest,
        preferred_element_type=jnp.float32,
    )
    rows_owned = weight.shape[0]
    summed_factor = lax.psum(factor, "dp")
    gram_matrix = jnp.dot(summed_factor, summed_factor.T, precision=highest)
    cholesky_factor = jnp.linalg.cholesky(gram_matrix)
    orth_basis = lax.linalg.triangular_solve(
        cholesky_factor, summed_factor, left_side=True, lower=True
    )
    own_basis = lax.dynamic_slice_in_dim(
        orth_basis, lax.axis_index("dp") * rows_owned, rows_owned, 1
    )
    local_second = jnp.dot(
        orth_basis, total_grad, precision=highest, preferred_element_type=jnp.float32
    )
    second = lax.psum(local_second, "dp")
    replicas = lax.axis_size("dp")
    low_rank = (
        lax.dot_general(
            orth_basis,
            second,
            (((0,), (0,)), ((), ())),
            precision=highest,
            preferred_element_type=jnp.float32,
        )
        / replicas
    )
    new_feedback = (total_grad - low_rank).astype(jnp.bfloat16)[None]
    update = (
        lax.dot_general(
            own_basis,
            second,
            (((0,), (0,)), ((), ())),
            precision=highest,
            preferred_element_type=jnp.float32,
        )
        / replicas
    )
    return (input_grads, new_feedback, update)


def solution(mesh):
    return jax.shard_map(
        local,
        mesh=mesh,
        in_specs=(
            P("dp", "tensor"),
            P("dp", "tensor"),
            P("dp", "tensor"),
            P(None, "tensor"),
            P("dp", None, "tensor"),
        ),
        out_specs=(P("dp", "tensor"), P("dp", None, "tensor"), P("dp", "tensor")),
        check_vma=False,
    )
```

profile of v0, /device:TPU:1, one launch (start us, length us, event | category | flops | bytes accessed | tf_op | source)
XLA Modules:
  0.0 593.5 jit_solution(14794718507124579374)
XLA Ops:
  7.2 0.0 copy-start
  7.2 0.0 copy-start.2
  7.2 0.0 all-reduce.4.cloned.1.call-start
  7.2 23.4 %all_gather.7 = bf16[128,3072]{1,0:T(8,128)(2,1)S(1)} all-gather(bf16[128,384]{1,0:T(8,128)(2,1)} %param.5), channel_id=1, replica_groups=mesh['dp'=64,'tensor'=8] {'tensor'}, dimensions={1}, use_global_device_ids=true | all-gather | bytes 884736 | tf_op jit(solution)/shard_map/all_gather | solution.py:10
  30.7 0.0 copy-done
  30.7 2.5 convert_add_fusion
  33.2 0.0 copy-start.1
  33.2 2.1 copy-done.1
  35.3 0.0 copy-done.2
  35.3 5.7 convolution_bitcast_fusion
  41.0 0.0 all-reduce.4.cloned.1.call-update
  41.0 0.0 all-reduce.6.cloned.1.call-start
  41.1 202.7 %all-reduce.4.cloned.1.call-done = f32[64,3072]{1,0:T(8,128)} async-done(((f32[64,3072]{1,0:T(8,128)}), f32[64,3072]{1,0:T(8,128)}) %all-reduce.4.cloned.1.call-update) | async-done | bytes 786448 | tf_op jit(solution)/shard_map/psum | solution.py:35
  243.8 2.2 fusion.8
  246.0 0.1 copy.8
  246.1 5.8 cholesky.16
  252.0 0.6 compare_reduce_fusion
  252.6 0.7 fusion.1
  253.3 4.9 custom-call.6
  258.2 2.0 fusion.2
  260.2 5.8 fusion.9
  265.9 0.0 all-reduce.6.cloned.1.call-update
  265.9 0.2 all-gather.2.cloned.1.call-start
  266.2 0.5 all-gather.2.cloned.1.call-update
  266.7 179.8 %all-reduce.6.cloned.1.call-done = f32[64,384]{1,0:T(8,128)} async-done(((f32[64,384]{1,0:T(8,128)}), f32[64,384]{1,0:T(8,128)}) %all-reduce.6.cloned.1.call-update) | async-done | bytes 98320 | tf_op jit(solution)/shard_map/psum | solution.py:47
  446.5 1.9 convolution_multiply_fusion
  448.4 7.1 %fusion = bf16[1,3072,384]{2,1,0:T(8,128)(2,1)} fusion(f32[3072,384]{1,0:T(8,128)} %copy-done.1, f32[64,3072]{1,0:T(8,128)S(1)} %fusion.2, f32[64,384]{1,0:T(8,128)} %all-reduce.6.cloned.1.call-done), kind=kOutput, calls=%fused_computation.2 | convolution fusion | flops 909508608 | bytes 7962624 | tf_op jit(solution)/shard_map/dot_general | solution.py:50
  455.4 76.2 %all-gather.2.cloned.1.call-done = bf16[3072,384]{1,0:T(8,128)(2,1)} async-done(((bf16[48,384]{1,0:T(8,128)(2,1)}), bf16[3072,384]{1,0:T(8,128)(2,1)}) %all-gather.2.cloned.1.call-update) | async-done | bytes 2359312 | tf_op jit(solution)/shard_map/all_gather | solution.py:17
  531.6 2.5 fusion.7
  534.2 52.2 %all-reduce.7 = bf16[128,3072]{1,0:T(8,128)(2,1)S(1)} all-reduce(f32[128,3072]{1,0:T(8,128)S(1)} %fusion.7), channel_id=1, replica_groups=mesh['dp'=64,'tensor'=8] {'tensor'}, use_global_device_ids=true, to_apply=%region_0.0 | all-reduce | flops 393216 | bytes 2359296 | tf_op jit(solution)/shard_map/psum | solution.py:22
  586.4 0.7 dynamic-slice_convert_fusion
  (2 shorter events, 0.0 us)
Async XLA Ops:
  7.2 23.5 %copy-start = (bf16[128,384]{1,0:T(8,128)(2,1)S(1)}, bf16[128,384]{1,0:T(8,128)(2,1)}, u32[]{:S(2)}) copy-start(bf16[128,384]{1,0:T(8,128)(2,1)} %param.6) | copy-start | bytes 294916
  7.2 28.1 %copy-start.2 = (f32[64,384]{1,0:T(8,128)S(1)}, f32[64,384]{1,0:T(8,128)}, u32[]{:S(2)}) copy-start(f32[64,384]{1,0:T(8,128)} %param.8) | copy-start | bytes 294916
  7.2 236.6 %all-reduce.4.cloned.1.call-start = ((), (), s32[]{:S(2)}) async-start(), calls=%async_computation.1 | async-start | bytes 1572864 | tf_op jit(solution)/shard_map/psum | solution.py:35
  33.2 2.1 copy-start.1
  41.0 405.5 %all-reduce.6.cloned.1.call-start = ((), (), s32[]{:S(2)}) async-start(), calls=%async_computation.2 | async-start | bytes 196608 | tf_op jit(solution)/shard_map/psum | solution.py:47
  265.9 265.7 %all-gather.2.cloned.1.call-start = ((), (), s32[]{:S(2)}) async-start(), calls=%async_computation | async-start | bytes 2396160 | tf_op jit(solution)/shard_map/all_gather | solution.py:17
Sparse Core Ops, SparseCore 0:
  41.2 202.6 all-reduce.3
  266.1 180.3 all-reduce.5
  450.3 81.2 all-gather.1
where the time goes:
time: 604 us; the launch traced here: 594 us
  waiting for transfers between devices  459 us (76%)
  blocking collectives  75.6 us (13%)
  matrix products  29.6 us (5%)
  between operations  13.8 us (2%)
  other arithmetic  12.1 us (2%)
    psum x1, waiting for transfers between devices, local(): summed_factor = lax.psum(factor, 'dp')  203 us
    psum x1, waiting for transfers between devices, local(): second = lax.psum(local_second, 'dp')  180 us
    all_gather x1, waiting for transfers between devices, local(): lax.all_gather(weight, 'dp', axis=0, tiled=True)  76.2 us
    psum x1, blocking collectives, local(): summed_inputs = lax.psum(partial_inputs, 'tensor')  52.2 us
    all_gather x1, blocking collectives, local(): lax.all_gather(acts, 'tensor', axis=1, tiled=True)  23.4 us
  transfers between devices with their start and end apart: 3, of which 3 were waited for; matrix products, arithmetic and copies ran while one was open for 2% of the time, Pallas kernels for 0%

commit v1 on v0

v1 whole, which is shorter than its diff:
```python
import jax
import jax.numpy as jnp
from jax import lax
from jax.experimental import pallas as pl
from jax.experimental.pallas import tpu as pltpu
from jax.sharding import PartitionSpec as P

MESH = pl.DeviceIdType.MESH
F32 = jnp.float32
BF16 = jnp.bfloat16
RANK = 64
TOK = 128
WIDTH = 384
NT = 8
NX, NZ, NC = 4, 8, 2
ROWS = 48
D = NT * WIDTH

NN = (((1,), (0,)), ((), ()))
NTD = (((1,), (1,)), ((), ()))
TN = (((0,), (0,)), ((), ()))


def mm(a, b, dims):
    return lax.dot_general(a, b, dims, preferred_element_type=F32)


def mm32(a, b, dims):
    return lax.dot_general(
        a, b, dims, precision=lax.Precision.HIGHEST, preferred_element_type=F32
    )


def pieces(value, n):
    parts = []
    for _ in range(n):
        top = value.astype(BF16)
        parts.append(top)
        value = value - top.astype(F32)
    return jnp.concatenate(parts, axis=0)


def folded(stack, n):
    rows = stack.shape[0] // n
    total = stack[(n - 1) * rows :]
    for i in range(n - 2, -1, -1):
        total = total + stack[i * rows : (i + 1) * rows]
    return total


def eliminate(a, first, last):
    rows = lax.broadcasted_iota(jnp.int32, (RANK, 1), 0)
    for j in range(first, last):
        scaled = a[j : j + 1, :] / a[j : j + 1, j : j + 1]
        column = jnp.where(rows > j, a[:, j : j + 1], 0.0)
        a = a - column * scaled
    return a


def kernel(
    acts, grads, weight, basis, fb_hbm,
    ig_out, nf_out, up_out,
    fb, acts_all, grads_all, wbuf, fp, rc, f1, rx, f2, rz, f_all, ft, t0, nf,
    sp, rs, rsz, sfull,
    fb_sem, nf_sem,
    ring_s, ring_r, gr_s, gr_r, spread_s, spread_r, wz_s, wz_r, wx_s, wx_r, wc_s, wc_r,
    fc_s, fc_r, fx_s, fx_r, fz_s, fz_r, az_s, az_r, ax_s, ax_r, ac_s, ac_r,
    sx_s, sx_r, sz_s, sz_r, sa_s, sa_r,
):
    dp = lax.axis_index("dp")
    y = lax.axis_index("tensor")
    c = dp % NC
    z = (dp // NC) % NZ
    x = dp // (NC * NZ)

    def at(x_, z_, c_):
        return (x_ * NZ + z_) * NC + c_

    q = c * NX + x
    group = dp // NT
    pair_dp = y * NT + dp % NT
    y_peers = [(dp, (y + k) % NT) for k in range(1, NT)]
    z_peers = [(at(x, (z + k) % NZ, c), y) for k in range(1, NZ)]
    xc_peers = [
        (at((x + (o % NX)) % NX, z, (c + o // NX) % NC), y) for o in range(1, NX * NC)
    ]
    partner = xc_peers[NX - 1]
    x_peers = xc_peers[: NX - 1]
    swaps = group != y

    sends = []

    def send(src, dst, ssem, rsem, peer):
        cp = pltpu.make_async_remote_copy(
            src_ref=src, dst_ref=dst, send_sem=ssem, recv_sem=rsem,
            device_id=peer, device_id_type=MESH,
        )
        cp.start()
        sends.append(cp)
        return cp

    barrier = pltpu.get_barrier_semaphore()
    for peer in y_peers + z_peers + xc_peers:
        pl.semaphore_signal(barrier, inc=1, device_id=peer, device_id_type=MESH)

    @pl.when(swaps)
    def _():
        pl.semaphore_signal(barrier, inc=1, device_id=(pair_dp, group), device_id_type=MESH)

    load = pltpu.make_async_copy(fb_hbm.at[0], fb, fb_sem)
    load.start()
    acts_all[y] = acts[...]
    grads_all[y] = grads[...]
    pl.semaphore_wait(barrier, 21 + jnp.where(swaps, 1, 0))

    right = (dp, (y + 1) % NT)
    left = (dp, (y + NT - 1) % NT)
    half = TOK // 2

    def ring(way, k, h, peer):
        slot = (y - k + NT) % NT if way == 0 else (y + k) % NT
        part = acts_all.at[slot, pl.ds(h * half, half)]
        return send(part, part, ring_s.at[way, k, h], ring_r.at[way, k, h], peer)

    hops = {}
    for h in range(2):
        hops[0, 0, h] = ring(0, 0, h, right)
        hops[1, 0, h] = ring(1, 0, h, left)

    bh, bc = (dp % NT) // NC, c
    mine = wbuf.at[group, bh, bc]
    swap = pltpu.make_async_remote_copy(
        src_ref=weight, dst_ref=wbuf.at[y, bh, bc], send_sem=spread_s, recv_sem=spread_r,
        device_id=(pair_dp, group), device_id_type=MESH,
    )

    @pl.when(swaps)
    def _():
        swap.start()

    @pl.when(jnp.logical_not(swaps))
    def _():
        wbuf[group, bh, bc] = weight[...]

    bs = pieces(basis[...], 3)
    hs = pieces(folded(mm(bs, grads[...], NTD), 3), 3)
    load.wait()
    for t in range(NT):
        fp[t] = folded(mm(bs, fb[t * WIDTH : (t + 1) * WIDTH], NTD), 3)

    core_cp, x_cp = {}, {}

    def block_of(k, way):
        return (y - k + NT) % NT if way == 0 else (y + k) % NT

    def add_acts(k, way):
        t = block_of(k, way)
        fp[t] = fp[t] + folded(mm(hs, acts_all[t], NN), 3)
        core_cp[k, way] = send(
            fp.at[t, pl.ds(32 * (1 - c), 32)], rc.at[t], fc_s.at[t], fc_r.at[t], partner
        )

    def x_stage(k, way):
        t = block_of(k, way)
        core_cp[k, way].wait_recv()
        f1[t] = fp[t, pl.ds(pl.multiple_of(32 * c, 32), 32)] + rc[t]
        for d in range(1, NX):
            to = (x + d) % NX
            x_cp[k, way, d] = send(
                f1.at[t, pl.ds(pl.multiple_of(8 * to, 8), 8)], rx.at[d - 1, t],
                fx_s.at[d - 1, t], fx_r.at[d - 1, t], x_peers[d - 1],
            )

    ways = {0: [0], 1: [0, 1], 2: [0, 1], 3: [0, 1], 4: [0]}
    for k in range(5):
        if k:
            for h in range(2):
                for way, peer in ((0, right), (1, left)):
                    if (way, k - 1, h) in hops:
                        hops[way, k - 1, h].wait_recv()
                        if k < 3 or (k == 3 and h == way):
                            hops[way, k, h] = ring(way, k, h, peer)
        for way in ways[k]:
            add_acts(k, way)
        if k == 1:
            @pl.when(swaps)
            def _():
                swap.wait()
            wz = [
                send(mine, mine, wz_s.at[i], wz_r.at[i], z_peers[i]) for i in range(NZ - 1)
            ]
        if k:
            for way in ways[k - 1]:
                x_stage(k - 1, way)

    gcp = [
        send(grads, grads_all.at[y], gr_s.at[i], gr_r.at[i], y_peers[i])
        for i in range(NT - 1)
    ]
    x_stage(4, 0)
    for t in range(NT):
        rows = pl.ds(t * WIDTH, WIDTH)
        t0[rows] = mm(acts_all[t], grads[...], TN) + fb[rows].astype(F32)
    for key in x_cp:
        x_cp[key].wait_recv()
    own = pl.ds(pl.multiple_of(8 * x, 8), 8)
    for t in range(NT):
        f2[t] = f1[t, own] + rx[0, t] + rx[1, t] + rx[2, t]
    fz = [
        send(f2.at[(z + i + 1) % NZ], rz.at[i], fz_s.at[i], fz_r.at[i], z_peers[i])
        for i in range(NZ - 1)
    ]
    for cp in wz:
        cp.wait_recv()
    wmine = wbuf.at[pl.ds(2 * x, 2), :, c]
    wx = [send(wmine, wmine, wx_s.at[i], wx_r.at[i], x_peers[i]) for i in range(NX - 1)]
    f3 = f2[z]
    for i in range(NZ - 1):
        fz[i].wait_recv()
        f3 = f3 + rz[i]

    top = f3.astype(BF16).astype(F32)
    f_all[z, q] = jnp.concatenate([top, f3 - top], axis=0).astype(BF16)
    az = [
        send(f_all.at[z, q], f_all.at[z, q], az_s.at[i], az_r.at[i], z_peers[i])
        for i in range(NZ - 1)
    ]
    for cp in az:
        cp.wait_recv()
    ax = [
        send(f_all.at[:, q], f_all.at[:, q], ax_s.at[i], ax_r.at[i], x_peers[i])
        for i in range(NX - 1)
    ]
    for cp in ax:
        cp.wait_recv()
    core_half = f_all.at[:, pl.ds(NX * c, NX)]
    ac = send(core_half, core_half, ac_s, ac_r, partner)
    ac.wait_recv()

    def unpaired(pairs):
        v = pairs.reshape(RANK // 8, 2, 8, pairs.shape[1])
        return (v[:, 0] + v[:, 1]).reshape(RANK, pairs.shape[1])

    through = jnp.zeros((2 * RANK, TOK), F32)
    direct = jnp.zeros((2 * RANK, WIDTH), F32)
    for t in range(NT):
        block = f_all[t].reshape(2 * RANK, WIDTH)
        through = through + mm(block, acts_all[t], NTD)
        direct = direct + mm(block, fb[t * WIDTH : (t + 1) * WIDTH], NN)
    local = unpaired(direct) + folded(mm(pieces(unpaired(through), 3), grads[...], NN), 3)
    sp[...] = local.reshape(RANK // 8, 8, WIDTH)
    sx = []
    for o in range(1, NX * NC):
        to = ((c + o // NX) % NC) * NX + (x + o % NX) % NX
        sx.append(
            send(sp.at[to], rs.at[o - 1], sx_s.at[o - 1], sx_r.at[o - 1], xc_peers[o - 1])
        )

    gram = jnp.zeros((2 * RANK, 2 * RANK), F32)
    for t in range(NT):
        block = f_all[t].reshape(2 * RANK, WIDTH)
        gram = gram + mm(block, block, NTD)
    lanes = lax.broadcasted_iota(jnp.int32, (2 * RANK, RANK), 0)
    cols = lax.broadcasted_iota(jnp.int32, (2 * RANK, RANK), 1)
    pick = jnp.where((lanes // 16) * 8 + lanes % 8 == cols, 1.0, 0.0)
    gram = mm32(unpaired(gram), pick, NN)
    eye = jnp.where(
        lax.broadcasted_iota(jnp.int32, (RANK, RANK), 0)
        == lax.broadcasted_iota(jnp.int32, (RANK, RANK), 1), 1.0, 0.0,
    )
    a = jnp.concatenate([gram, eye], axis=1)
    a = eliminate(a, 0, 12)

    s1 = sp[q]
    for i in range(NX * NC - 1):
        sx[i].wait_recv()
        s1 = s1 + rs[i]
    rsz[z] = s1
    sz = [
        send(rsz.at[z], rsz.at[z], sz_s.at[i], sz_r.at[i], z_peers[i]) for i in range(NZ - 1)
    ]
    a = eliminate(a, 12, 44)
    for cp in sz:
        cp.wait_recv()
    s2 = rsz[0]
    for i in range(1, NZ):
        s2 = s2 + rsz[i]
    sfull[q] = s2
    sa = [
        send(sfull.at[q], sfull.at[q], sa_s.at[i], sa_r.at[i], xc_peers[i])
        for i in range(NX * NC - 1)
    ]
    a = eliminate(a, 44, RANK)
    for t in range(NT):
        ft[pl.ds(t * WIDTH, WIDTH)] = (
            f_all[t].reshape(2 * RANK, WIDTH).astype(F32).T.astype(BF16)
        )
    pivots = jnp.sum(a[:, :RANK] * eye, axis=1, keepdims=True)
    inverse = a[:, RANK:]
    for cp in wx:
        cp.wait_recv()
    whalf = wbuf.at[:, :, c]
    wc = send(whalf, whalf, wc_s, wc_r, partner)
    for cp in sa:
        cp.wait_recv()

    solved = mm32(inverse, sfull[...].reshape(RANK, WIDTH), NN) / (pivots * 64.0)
    coef = mm32(inverse, solved, TN)
    ctop = coef.astype(BF16).astype(F32)

    def doubled(v):
        v = v.reshape(RANK // 8, 1, 8, WIDTH)
        return jnp.concatenate([v, v], axis=1).reshape(2 * RANK, WIDTH).astype(BF16)

    c1, c2 = doubled(ctop), doubled(coef - ctop)

    def low_rank(rows):
        left_side = ft[rows]
        return mm(left_side, c1, NN) + mm(left_side, c2, NN)

    stores = []
    for t in range(NT):
        rows = pl.ds(t * WIDTH, WIDTH)
        nf[rows] = (t0[rows] - low_rank(rows)).astype(BF16)
        cp = pltpu.make_async_copy(nf.at[rows], nf_out.at[0, rows], nf_sem.at[t])
        cp.start()
        stores.append(cp)
    up_out[...] = low_rank(pl.ds(pl.multiple_of(dp * ROWS, 16), ROWS))

    for cp in gcp:
        cp.wait_recv()
    wc.wait_recv()
    out = jnp.zeros((TOK, WIDTH), F32)
    for j in range(NT):
        out = out + mm(grads_all[j], wbuf[j].reshape(WIDTH, WIDTH), NTD)
    ig_out[...] = out.astype(BF16)

    for cp in stores:
        cp.wait()
    for cp in sends:
        cp.wait_send()


def local(acts, grads_out, weight, basis_init, feedback):
    vmem = pl.BlockSpec(memory_space=pltpu.VMEM)
    hbm = pl.BlockSpec(memory_space=pl.ANY)
    dma = pltpu.SemaphoreType.DMA
    scratch = [
        pltpu.VMEM((D, WIDTH), BF16),
        pltpu.VMEM((NT, TOK, WIDTH), BF16),
        pltpu.VMEM((NT, TOK, WIDTH), BF16),
        pltpu.VMEM((NT, 4, NC, ROWS, WIDTH), BF16),
        pltpu.VMEM((NT, RANK, WIDTH), F32),
        pltpu.VMEM((NT, RANK // 2, WIDTH), F32),
        pltpu.VMEM((NT, RANK // 2, WIDTH), F32),
        pltpu.VMEM((NX - 1, NT, 8, WIDTH), F32),
        pltpu.VMEM((NT, 8, WIDTH), F32),
        pltpu.VMEM((NZ - 1, 8, WIDTH), F32),
        pltpu.VMEM((NT, NX * NC, 16, WIDTH), BF16),
        pltpu.VMEM((D, 2 * RANK), BF16),
        pltpu.VMEM((D, WIDTH), F32),
        pltpu.VMEM((D, WIDTH), BF16),
        pltpu.VMEM((NX * NC, 8, WIDTH), F32),
        pltpu.VMEM((NX * NC - 1, 8, WIDTH), F32),
        pltpu.VMEM((NZ, 8, WIDTH), F32),
        pltpu.VMEM((NX * NC, 8, WIDTH), F32),
        dma, dma((NT,)),
        dma((2, 4, 2)), dma((2, 4, 2)),
        dma((NT - 1,)), dma((NT - 1,)),
        dma, dma,
        dma((NZ - 1,)), dma((NZ - 1,)),
        dma((NX - 1,)), dma((NX - 1,)),
        dma, dma,
        dma((NT,)), dma((NT,)),
        dma((NX - 1, NT)), dma((NX - 1, NT)),
        dma((NZ - 1,)), dma((NZ - 1,)),
        dma((NZ - 1,)), dma((NZ - 1,)),
        dma((NX - 1,)), dma((NX - 1,)),
        dma, dma,
        dma((NX * NC - 1,)), dma((NX * NC - 1,)),
        dma((NZ - 1,)), dma((NZ - 1,)),
        dma((NX * NC - 1,)), dma((NX * NC - 1,)),
    ]
    return pl.pallas_call(
        kernel,
        out_shape=(
            jax.ShapeDtypeStruct((TOK, WIDTH), BF16),
            jax.ShapeDtypeStruct((1, D, WIDTH), BF16),
            jax.ShapeDtypeStruct((ROWS, WIDTH), F32),
        ),
        in_specs=[vmem, vmem, vmem, vmem, hbm],
        out_specs=(vmem, hbm, vmem),
        scratch_shapes=scratch,
        compiler_params=pltpu.CompilerParams(
            collective_id=0, has_side_effects=True, vmem_limit_bytes=48 * 1024 * 1024
        ),
    )(acts, grads_out, weight, basis_init, feedback)


def solution(mesh):
    return jax.shard_map(
        local,
        mesh=mesh,
        in_specs=(
            P("dp", "tensor"),
            P("dp", "tensor"),
            P("dp", "tensor"),
            P(None, "tensor"),
            P("dp", None, "tensor"),
        ),
        out_specs=(P("dp", "tensor"), P("dp", None, "tensor"), P("dp", "tensor")),
        check_vma=False,
    )
```

time: 604 us -> 95.5 us (0.16); the launches traced: 594 us -> 95.2 us
  waiting for transfers between devices: 459 us -> 0 us
  Pallas kernels: 0 us -> 86.7 us
  blocking collectives: 75.6 us -> 0 us
  matrix products: 29.6 us -> 0 us
  between operations: 13.8 us -> 0.65 us
  other arithmetic: 12.1 us -> 0 us
    psum x2 -> x0, waiting for transfers between devices: 383 us -> none  [the longest x1 203 us: local(): summed_factor = lax.psum(factor, 'dp')]
    pallas_call x0 -> x1, Pallas kernels: none -> 86.7 us  [local(): pl.pallas_call(kernel, out_shape=(jax.ShapeDtypeStruct((TOK, WIDTH), BF16...]
    all_gather x1 -> x0, waiting for transfers between devices: 76.2 us -> none  [local(): lax.all_gather(weight, 'dp', axis=0, tiled=True)]
    psum x1 -> x0, blocking collectives: 52.2 us -> none  [local(): summed_inputs = lax.psum(partial_inputs, 'tensor')]
    dot_general x7 -> x0, matrix products: 27.6 us -> none  [the longest x1 7.07 us: local(): lax.dot_general(orth_basis, second, (((0,), (0,)), ((), ())), precision=h...]
    all_gather x1 -> x0, blocking collectives: 23.4 us -> none  [local(): lax.all_gather(acts, 'tensor', axis=1, tiled=True)]
    another operation x5 -> x0, other arithmetic: 12.1 us -> none  [the longest x3 6.52 us: local(): cholesky_factor = jnp.linalg.cholesky(gram_matrix)]
  transfers between devices with their start and end apart: 3 -> 0, of which waited for: 3 -> 0; matrix products, arithmetic and copies ran while one was open for 2% -> 0% of each run, Pallas kernels for 0% -> 0%
where the time goes in v1:
time: 95.5 us; the launch traced here: 95.2 us
  Pallas kernels  86.7 us (91%)
  local copies, waits for them, and re-layouts  7.78 us (8%)
    pallas_call x1, Pallas kernels, local(): pl.pallas_call(kernel, out_shape=(jax.ShapeDtypeStruct((TOK, WIDTH), BF16...  86.7 us
    unnamed x13, local copies, waits for them, and re-layouts  7.78 us

profile of v1, /device:TPU:1, one launch (start us, length us, event | category | flops | bytes accessed | tf_op | source)
XLA Modules:
  0.0 95.2 jit_solution(16930347876767798994)
XLA Ops:
  0.6 0.0 copy-start
  0.6 1.7 %copy-done = bf16[1,3072,384]{2,1,0:T(8,128)(2,1)S(1)} copy-done((bf16[1,3072,384]{2,1,0:T(8,128)(2,1)S(1)}, bf16[1,3072,384]{2,1,0:T(8,128)(2,1)}, u32[]{:S(2)}) %copy-start) | copy-done | bytes 2359320
  2.3 0.0 copy-start.1
  2.3 0.9 copy-done.1
  3.2 0.0 copy-start.2
  3.2 0.9 copy-done.2
  4.1 0.0 copy-start.3
  4.1 0.9 copy-done.3
  5.0 0.0 copy-start.4
  5.0 0.8 copy-done.4
  5.7 86.7 %shard_map.76 = (bf16[128,384]{1,0:T(8,128)(2,1)S(1)}, bf16[1,3072,384]{2,1,0:T(8,128)(2,1)S(1)}, f32[48,384]{1,0:T(8,128)S(1)}) custom-call(bf16[128,384]{1,0:T(8,128)(2,1)S(1)} %copy-done.1, bf16[128,384]{1,0:T(8,128)(2,1)S(1)} %copy-done.2, bf16[48,384]{1,0:T(8,128)(2,1)S(1)} %copy-done.4, f32[64,384]{1,0:T(8,128)S(1)} %copy-done.3, ...), custom_call_target="tpu_custom_call" | custom-call | tf_op jit(solution)/shard_map/pallas_call | solution.py:384
  92.5 0.6 copy.11
  93.1 1.4 %copy.12 = bf16[1,3072,384]{2,1,0:T(8,128)(2,1)} copy(bf16[1,3072,384]{2,1,0:T(8,128)(2,1)S(1)} %get-tuple-element.7) | data formatting | bytes 4718592
  94.5 0.6 copy.13
Async XLA Ops:
  0.6 1.7 %copy-start = (bf16[1,3072,384]{2,1,0:T(8,128)(2,1)S(1)}, bf16[1,3072,384]{2,1,0:T(8,128)(2,1)}, u32[]{:S(2)}) copy-start(bf16[1,3072,384]{2,1,0:T(8,128)(2,1)} %fb_hbm.1) | copy-start | bytes 7077892
  2.3 0.9 copy-start.1
  3.2 0.9 copy-start.2
  4.1 0.9 copy-start.3
  5.0 0.8 copy-start.4

commit v2 on v1

--- a/solution.py
+++ b/solution.py
@@ -58,12 +58,12 @@
 
 
 def kernel(
-    acts, grads, weight, basis, fb_hbm,
-    ig_out, nf_out, up_out,
-    fb, acts_all, grads_all, wbuf, fp, rc, f1, rx, f2, rz, f_all, ft, t0, nf,
+    acts_hbm, grads_hbm, weight_hbm, basis_hbm, fb_hbm,
+    ig_out, t0, ft, coefs,
+    grads, weight, basis, fb, acts_all, grads_all, wbuf, fp, rc, f1, rx, f2, rz, f_all,
     sp, rs, rsz, sfull,
-    fb_sem, nf_sem,
-    ring_s, ring_r, gr_s, gr_r, spread_s, spread_r, wz_s, wz_r, wx_s, wx_r, wc_s, wc_r,
+    in_sem,
+    ring_s, ring_r, gr_s, gr_r, spread_s, spread_r, wz_s, wz_r, wx_s, wx_r, wy_s, wy_r, wc_s, wc_r,
     fc_s, fc_r, fx_s, fx_r, fz_s, fz_r, az_s, az_r, ax_s, ax_r, ac_s, ac_r,
     sx_s, sx_r, sz_s, sz_r, sa_s, sa_r,
 ):
@@ -107,25 +107,20 @@
     def _():
         pl.semaphore_signal(barrier, inc=1, device_id=(pair_dp, group), device_id_type=MESH)
 
-    load = pltpu.make_async_copy(fb_hbm.at[0], fb, fb_sem)
-    load.start()
-    acts_all[y] = acts[...]
-    grads_all[y] = grads[...]
+    loads = [
+        pltpu.make_async_copy(src, dst, in_sem.at[i])
+        for i, (src, dst) in enumerate([
+            (acts_hbm, acts_all.at[y]), (weight_hbm, weight), (grads_hbm, grads),
+            (basis_hbm, basis),
+        ] + [
+            (fb_hbm.at[0, pl.ds(t * WIDTH, WIDTH)], fb.at[t]) for t in range(NT)
+        ])
+    ]
+    for cp in loads:
+        cp.start()
+    loads[0].wait()
+    loads[1].wait()
     pl.semaphore_wait(barrier, 21 + jnp.where(swaps, 1, 0))
-
-    right = (dp, (y + 1) % NT)
-    left = (dp, (y + NT - 1) % NT)
-    half = TOK // 2
-
-    def ring(way, k, h, peer):
-        slot = (y - k + NT) % NT if way == 0 else (y + k) % NT
-        part = acts_all.at[slot, pl.ds(h * half, half)]
-        return send(part, part, ring_s.at[way, k, h], ring_r.at[way, k, h], peer)
-
-    hops = {}
-    for h in range(2):
-        hops[0, 0, h] = ring(0, 0, h, right)
-        hops[1, 0, h] = ring(1, 0, h, left)
 
     bh, bc = (dp % NT) // NC, c
     mine = wbuf.at[group, bh, bc]
@@ -142,16 +137,29 @@
     def _():
         wbuf[group, bh, bc] = weight[...]
 
+    right = (dp, (y + 1) % NT)
+    left = (dp, (y + NT - 1) % NT)
+    quarter = TOK // 4
+
+    def block_of(k, way):
+        return (y - k + NT) % NT if way == 0 else (y + k) % NT
+
+    def ring(way, k, h, peer):
+        part = acts_all.at[block_of(k, way), pl.ds(h * quarter, quarter)]
+        return send(part, part, ring_s.at[way, k, h], ring_r.at[way, k, h], peer)
+
+    hops = {}
+    for h in range(4):
+        hops[0, 0, h] = ring(0, 0, h, right)
+        hops[1, 0, h] = ring(1, 0, h, left)
+
+    loads[2].wait()
+    loads[3].wait()
+    grads_all[y] = grads[...]
     bs = pieces(basis[...], 3)
     hs = pieces(folded(mm(bs, grads[...], NTD), 3), 3)
-    load.wait()
-    for t in range(NT):
-        fp[t] = folded(mm(bs, fb[t * WIDTH : (t + 1) * WIDTH], NTD), 3)
 
     core_cp, x_cp = {}, {}
-
-    def block_of(k, way):
-        return (y - k + NT) % NT if way == 0 else (y + k) % NT
 
     def add_acts(k, way):
         t = block_of(k, way)
@@ -171,52 +179,80 @@
                 fx_s.at[d - 1, t], fx_r.at[d - 1, t], x_peers[d - 1],
             )
 
+    own = pl.ds(pl.multiple_of(8 * x, 8), 8)
+
+    def z_stage(k, way):
+        t = block_of(k, way)
+        for d in range(1, NX):
+            x_cp[k, way, d].wait_recv()
+        f2[t] = f1[t, own] + rx[0, t] + rx[1, t] + rx[2, t]
+        away = (t - z + NZ) % NZ
+
+        @pl.when(away != 0)
+        def _():
+            z_copy(t, away).start()
+
+    def z_copy(t, away):
+        return pltpu.make_async_remote_copy(
+            src_ref=f2.at[t], dst_ref=rz.at[away - 1], send_sem=fz_s.at[away - 1],
+            recv_sem=fz_r.at[away - 1], device_id=(at(x, t, c), y), device_id_type=MESH,
+        )
+
     ways = {0: [0], 1: [0, 1], 2: [0, 1], 3: [0, 1], 4: [0]}
     for k in range(5):
         if k:
-            for h in range(2):
+            for h in range(4):
                 for way, peer in ((0, right), (1, left)):
                     if (way, k - 1, h) in hops:
                         hops[way, k - 1, h].wait_recv()
-                        if k < 3 or (k == 3 and h == way):
+                        if k < 3 or (k == 3 and h // 2 == way):
                             hops[way, k, h] = ring(way, k, h, peer)
+        if k == 0:
+            continue
+        if k == 1:
+            for cp in loads[4:]:
+                cp.wait()
+            for t in range(NT):
+                fp[t] = folded(mm(bs, fb[t], NTD), 3)
+            add_acts(0, 0)
         for way in ways[k]:
             add_acts(k, way)
-        if k == 1:
+        if k == 2:
             @pl.when(swaps)
             def _():
                 swap.wait()
             wz = [
                 send(mine, mine, wz_s.at[i], wz_r.at[i], z_peers[i]) for i in range(NZ - 1)
             ]
-        if k:
+        if k >= 1:
             for way in ways[k - 1]:
                 x_stage(k - 1, way)
+        if k >= 3:
+            for way in ways[k - 3]:
+                z_stage(k - 3, way)
 
     gcp = [
         send(grads, grads_all.at[y], gr_s.at[i], gr_r.at[i], y_peers[i])
         for i in range(NT - 1)
     ]
     x_stage(4, 0)
+    for k in (2, 3):
+        for way in ways[k]:
+            z_stage(k, way)
     for t in range(NT):
-        rows = pl.ds(t * WIDTH, WIDTH)
-        t0[rows] = mm(acts_all[t], grads[...], TN) + fb[rows].astype(F32)
-    for key in x_cp:
-        x_cp[key].wait_recv()
-    own = pl.ds(pl.multiple_of(8 * x, 8), 8)
-    for t in range(NT):
-        f2[t] = f1[t, own] + rx[0, t] + rx[1, t] + rx[2, t]
-    fz = [
-        send(f2.at[(z + i + 1) % NZ], rz.at[i], fz_s.at[i], fz_r.at[i], z_peers[i])
-        for i in range(NZ - 1)
-    ]
+        t0[t] = mm(acts_all[t], grads[...], TN) + fb[t].astype(F32)
+    z_stage(4, 0)
     for cp in wz:
         cp.wait_recv()
     wmine = wbuf.at[pl.ds(2 * x, 2), :, c]
-    wx = [send(wmine, wmine, wx_s.at[i], wx_r.at[i], x_peers[i]) for i in range(NX - 1)]
+    wx = {
+        way: send(wmine, wmine, wx_s.at[way], wx_r.at[way], x_peers[(0, NX - 2)[way]])
+        for way in (0, 1)
+    }
     f3 = f2[z]
+    zsum = [z_copy((z + i) % NZ, i) for i in range(1, NZ)]
     for i in range(NZ - 1):
-        fz[i].wait_recv()
+        zsum[i].wait_recv()
         f3 = f3 + rz[i]
 
     top = f3.astype(BF16).astype(F32)
@@ -225,17 +261,16 @@
         send(f_all.at[z, q], f_all.at[z, q], az_s.at[i], az_r.at[i], z_peers[i])
         for i in range(NZ - 1)
     ]
-    for cp in az:
-        cp.wait_recv()
-    ax = [
-        send(f_all.at[:, q], f_all.at[:, q], ax_s.at[i], ax_r.at[i], x_peers[i])
-        for i in range(NX - 1)
-    ]
-    for cp in ax:
-        cp.wait_recv()
-    core_half = f_all.at[:, pl.ds(NX * c, NX)]
-    ac = send(core_half, core_half, ac_s, ac_r, partner)
-    ac.wait_recv()
+    ax, ac = {}, {}
+    order = [0, 1, 7, 2, 6, 3, 5, 4]
+    for o in order:
+        zb = (z - o + NZ) % NZ
+        if o:
+            az[o - 1].wait_recv()
+        for i in range(NX - 1):
+            ax[o, i] = send(
+                f_all.at[zb, q], f_all.at[zb, q], ax_s.at[i, zb], ax_r.at[i, zb], x_peers[i]
+            )
 
     def unpaired(pairs):
         v = pairs.reshape(RANK // 8, 2, 8, pairs.shape[1])
@@ -243,10 +278,20 @@
 
     through = jnp.zeros((2 * RANK, TOK), F32)
     direct = jnp.zeros((2 * RANK, WIDTH), F32)
-    for t in range(NT):
-        block = f_all[t].reshape(2 * RANK, WIDTH)
-        through = through + mm(block, acts_all[t], NTD)
-        direct = direct + mm(block, fb[t * WIDTH : (t + 1) * WIDTH], NN)
+    for o in order:
+        zb = (z - o + NZ) % NZ
+        for i in range(NX - 1):
+            ax[o, i].wait_recv()
+        part = f_all.at[zb, pl.ds(NX * c, NX)]
+        ac[o] = send(part, part, ac_s.at[zb], ac_r.at[zb], partner)
+    for some in (order[:4], order[4:]):
+        for o in some:
+            ac[o].wait_recv()
+        for o in some:
+            zb = (z - o + NZ) % NZ
+            block = f_all[zb].reshape(2 * RANK, WIDTH)
+            through = through + mm(block, acts_all[zb], NTD)
+            direct = direct + mm(block, fb[zb], NN)
     local = unpaired(direct) + folded(mm(pieces(unpaired(through), 3), grads[...], NN), 3)
     sp[...] = local.reshape(RANK // 8, 8, WIDTH)
     sx = []
@@ -256,6 +301,11 @@
             send(sp.at[to], rs.at[o - 1], sx_s.at[o - 1], sx_r.at[o - 1], xc_peers[o - 1])
         )
 
+    wy = {}
+    for way in (0, 1):
+        wx[way].wait_recv()
+        part = wbuf.at[2 * ((x + (3, 1)[way]) % NX) + way, :, c]
+        wy[way] = send(part, part, wy_s.at[way], wy_r.at[way], x_peers[(0, NX - 2)[way]])
     gram = jnp.zeros((2 * RANK, 2 * RANK), F32)
     for t in range(NT):
         block = f_all[t].reshape(2 * RANK, WIDTH)
@@ -282,6 +332,10 @@
     a = eliminate(a, 12, 44)
     for cp in sz:
         cp.wait_recv()
+    for way in (0, 1):
+        wy[way].wait_recv()
+    whalf = wbuf.at[:, :, c]
+    wc = send(whalf, whalf, wc_s, wc_r, partner)
     s2 = rsz[0]
     for i in range(1, NZ):
         s2 = s2 + rsz[i]
@@ -292,41 +346,11 @@
     ]
     a = eliminate(a, 44, RANK)
     for t in range(NT):
-        ft[pl.ds(t * WIDTH, WIDTH)] = (
+        ft[t] = (
             f_all[t].reshape(2 * RANK, WIDTH).astype(F32).T.astype(BF16)
         )
     pivots = jnp.sum(a[:, :RANK] * eye, axis=1, keepdims=True)
     inverse = a[:, RANK:]
-    for cp in wx:
-        cp.wait_recv()
-    whalf = wbuf.at[:, :, c]
-    wc = send(whalf, whalf, wc_s, wc_r, partner)
-    for cp in sa:
-        cp.wait_recv()
-
-    solved = mm32(inverse, sfull[...].reshape(RANK, WIDTH), NN) / (pivots * 64.0)
-    coef = mm32(inverse, solved, TN)
-    ctop = coef.astype(BF16).astype(F32)
-
-    def doubled(v):
-        v = v.reshape(RANK // 8, 1, 8, WIDTH)
-        return jnp.concatenate([v, v], axis=1).reshape(2 * RANK, WIDTH).astype(BF16)
-
-    c1, c2 = doubled(ctop), doubled(coef - ctop)
-
-    def low_rank(rows):
-        left_side = ft[rows]
-        return mm(left_side, c1, NN) + mm(left_side, c2, NN)
-
-    stores = []
-    for t in range(NT):
-        rows = pl.ds(t * WIDTH, WIDTH)
-        nf[rows] = (t0[rows] - low_rank(rows)).astype(BF16)
-        cp = pltpu.make_async_copy(nf.at[rows], nf_out.at[0, rows], nf_sem.at[t])
-        cp.start()
-        stores.append(cp)
-    up_out[...] = low_rank(pl.ds(pl.multiple_of(dp * ROWS, 16), ROWS))
-
     for cp in gcp:
         cp.wait_recv()
     wc.wait_recv()
@@ -335,18 +359,55 @@
         out = out + mm(grads_all[j], wbuf[j].reshape(WIDTH, WIDTH), NTD)
     ig_out[...] = out.astype(BF16)
 
+    for cp in sa:
+        cp.wait_recv()
+
+    solved = mm32(inverse, sfull[...].reshape(RANK, WIDTH), NN) / (pivots * 64.0)
+    coef = mm32(inverse, solved, TN)
+    ctop = coef.astype(BF16).astype(F32)
+
+    def doubled(v):
+        v = v.reshape(RANK // 8, 1, 8, WIDTH)
+        return jnp.concatenate([v, v], axis=1).reshape(2 * RANK, WIDTH).astype(BF16)
+
+    coefs[0], coefs[1] = doubled(ctop), doubled(coef - ctop)
+
+    for cp in sends:
+        cp.wait_send()
+    for cp in zsum:
+        cp.wait_send()
+
+
+def finish(t0, ft, coefs, ig, ig_out, nf_out, up_out, nf, up, sems):
+    def low_rank(left_side):
+        return mm(left_side, coefs[0], NN) + mm(left_side, coefs[1], NN)
+
+    stores = [pltpu.make_async_copy(ig, ig_out, sems.at[NT])]
+    stores[0].start()
+    dp = lax.axis_index("dp")
+    first = pl.multiple_of((dp % NT) * ROWS, 16)
+    up[...] = low_rank(ft[dp // NT, pl.ds(first, ROWS)])
+    stores.append(pltpu.make_async_copy(up, up_out, sems.at[NT + 1]))
+    stores[1].start()
+    for t in range(NT):
+        nf[t] = (t0[t] - low_rank(ft[t])).astype(BF16)
+        stores.append(
+            pltpu.make_async_copy(nf.at[t], nf_out.at[0, pl.ds(t * WIDTH, WIDTH)], sems.at[t])
+        )
+        stores[-1].start()
     for cp in stores:
         cp.wait()
-    for cp in sends:
-        cp.wait_send()
 
 
 def local(acts, grads_out, weight, basis_init, feedback):
     vmem = pl.BlockSpec(memory_space=pltpu.VMEM)
-    hbm = pl.BlockSpec(memory_space=pl.ANY)
+    hbm = pl.BlockSpec(memory_space=pltpu.HBM)
     dma = pltpu.SemaphoreType.DMA
     scratch = [
-        pltpu.VMEM((D, WIDTH), BF16),
+        pltpu.VMEM((TOK, WIDTH), BF16),
+        pltpu.VMEM((ROWS, WIDTH), BF16),
+        pltpu.VMEM((RANK, WIDTH), F32),
+        pltpu.VMEM((NT, WIDTH, WIDTH), BF16),
         pltpu.VMEM((NT, TOK, WIDTH), BF16),
         pltpu.VMEM((NT, TOK, WIDTH), BF16),
         pltpu.VMEM((NT, 4, NC, ROWS, WIDTH), BF16),
@@ -357,44 +418,63 @@
         pltpu.VMEM((NT, 8, WIDTH), F32),
         pltpu.VMEM((NZ - 1, 8, WIDTH), F32),
         pltpu.VMEM((NT, NX * NC, 16, WIDTH), BF16),
-        pltpu.VMEM((D, 2 * RANK), BF16),
-        pltpu.VMEM((D, WIDTH), F32),
-        pltpu.VMEM((D, WIDTH), BF16),
         pltpu.VMEM((NX * NC, 8, WIDTH), F32),
         pltpu.VMEM((NX * NC - 1, 8, WIDTH), F32),
         pltpu.VMEM((NZ, 8, WIDTH), F32),
         pltpu.VMEM((NX * NC, 8, WIDTH), F32),
-        dma, dma((NT,)),
-        dma((2, 4, 2)), dma((2, 4, 2)),
+        dma((4 + NT,)),
+        dma((2, 4, 4)), dma((2, 4, 4)),
         dma((NT - 1,)), dma((NT - 1,)),
         dma, dma,
         dma((NZ - 1,)), dma((NZ - 1,)),
-        dma((NX - 1,)), dma((NX - 1,)),
+        dma((2,)), dma((2,)),
+        dma((2,)), dma((2,)),
         dma, dma,
         dma((NT,)), dma((NT,)),
         dma((NX - 1, NT)), dma((NX - 1, NT)),
         dma((NZ - 1,)), dma((NZ - 1,)),
         dma((NZ - 1,)), dma((NZ - 1,)),
-        dma((NX - 1,)), dma((NX - 1,)),
-        dma, dma,
+        dma((NX - 1, NZ)), dma((NX - 1, NZ)),
+        dma((NZ,)), dma((NZ,)),
         dma((NX * NC - 1,)), dma((NX * NC - 1,)),
         dma((NZ - 1,)), dma((NZ - 1,)),
         dma((NX * NC - 1,)), dma((NX * NC - 1,)),
     ]
+    parts = pl.pallas_call(
+        kernel,
+        out_shape=(
+            jax.ShapeDtypeStruct((TOK, WIDTH), BF16),
+            jax.ShapeDtypeStruct((NT, WIDTH, WIDTH), F32),
+            jax.ShapeDtypeStruct((NT, WIDTH, 2 * RANK), BF16),
+            jax.ShapeDtypeStruct((2, 2 * RANK, WIDTH), BF16),
+        ),
+        in_specs=[hbm] * 5,
+        out_specs=(vmem,) * 4,
+        scratch_shapes=scratch,
+        compiler_params=pltpu.CompilerParams(
+            collective_id=0, has_side_effects=True, vmem_limit_bytes=32 * 1024 * 1024
+        ),
+    )(*(
+        pltpu.with_memory_space_constraint(v, pltpu.HBM)
+        for v in (acts, grads_out, weight, basis_init, feedback)
+    ))
+    input_grads, total, factor_t, coefs = parts
     return pl.pallas_call(
-        kernel,
+        finish,
         out_shape=(
             jax.ShapeDtypeStruct((TOK, WIDTH), BF16),
             jax.ShapeDtypeStruct((1, D, WIDTH), BF16),
             jax.ShapeDtypeStruct((ROWS, WIDTH), F32),
         ),
-        in_specs=[vmem, vmem, vmem, vmem, hbm],
-        out_specs=(vmem, hbm, vmem),
-        scratch_shapes=scratch,
-        compiler_params=pltpu.CompilerParams(
-            collective_id=0, has_side_effects=True, vmem_limit_bytes=48 * 1024 * 1024
-        ),
-    )(acts, grads_out, weight, basis_init, feedback)
+        in_specs=[vmem] * 4,
+        out_specs=(hbm,) * 3,
+        scratch_shapes=[
+            pltpu.VMEM((NT, WIDTH, WIDTH), BF16),
+            pltpu.VMEM((ROWS, WIDTH), F32),
+            dma((NT + 2,)),
+        ],
+        compiler_params=pltpu.CompilerParams(vmem_limit_bytes=20 * 1024 * 1024),
+    )(total, factor_t, coefs, input_grads)
 
 
 def solution(mesh):

time: 95.5 us -> 74.9 us (0.78)
  Pallas kernels: 86.7 us -> 74.1 us
  local copies, waits for them, and re-layouts: 7.78 us -> 0 us
    pallas_call x1, Pallas kernels: 86.7 us -> 71.9 us  [local(): pl.pallas_call(kernel, out_shape=(jax.ShapeDtypeStruct((TOK, WIDTH), BF16...]
    unnamed x13 -> x0, local copies, waits for them, and re-layouts: 7.78 us -> none
    pallas_call x0 -> x1, Pallas kernels: none -> 2.22 us  [local(): pl.pallas_call(finish, out_shape=(jax.ShapeDtypeStruct((TOK, WIDTH), BF16...]
where the time goes in v2:
time: 74.9 us; the launch traced here: 74.8 us
  Pallas kernels  74.1 us (99%)
    pallas_call x1, Pallas kernels, local(): pl.pallas_call(kernel, out_shape=(jax.ShapeDtypeStruct((TOK, WIDTH), BF16...  71.9 us
    pallas_call x1, Pallas kernels, local(): pl.pallas_call(finish, out_shape=(jax.ShapeDtypeStruct((TOK, WIDTH), BF16...  2.22 us

profile of v2, /device:TPU:1, one launch (start us, length us, event | category | flops | bytes accessed | tf_op | source)
XLA Modules:
  0.0 74.8 jit_solution(8285455177658419225)
XLA Ops:
  0.6 71.9 %shard_map.76 = (bf16[128,384]{1,0:T(8,128)(2,1)S(1)}, f32[8,384,384]{2,1,0:T(8,128)S(1)}, bf16[8,384,128]{2,1,0:T(8,128)(2,1)S(1)}, bf16[2,128,384]{2,1,0:T(8,128)(2,1)S(1)}) custom-call(bf16[128,384]{1,0:T(8,128)(2,1)} %acts_hbm.1, bf16[128,384]{1,0:T(8,128)(2,1)} %grads_hbm.1, bf16[48,384]{1,0:T(8,128)(2,1)} %weight_hbm.1, f32[64,384]{1,0:T(8,128)} %basis_hbm.1, ...), custom_call_target="tpu_custom_call" | custom-call | tf_op jit(solution)/shard_map/pallas_call | solution.py:443
  72.5 2.2 %shard_map.77 = (bf16[128,384]{1,0:T(8,128)(2,1)}, bf16[1,3072,384]{2,1,0:T(8,128)(2,1)}, f32[48,384]{1,0:T(8,128)}) custom-call(f32[8,384,384]{2,1,0:T(8,128)S(1)} %get-tuple-element.7.t0, bf16[8,384,128]{2,1,0:T(8,128)(2,1)S(1)} %get-tuple-element.8.ft, bf16[2,128,384]{2,1,0:T(8,128)(2,1)S(1)} %get-tuple-element.9.coefs, ...), custom_call_target="tpu_custom_call" | custom-call | tf_op jit(solution)/shard_map/pallas_call | solution.py:462

commit v3 on v2

--- a/solution.py
+++ b/solution.py
@@ -63,9 +63,8 @@
     grads, weight, basis, fb, acts_all, grads_all, wbuf, fp, rc, f1, rx, f2, rz, f_all,
     sp, rs, rsz, sfull,
     in_sem,
-    ring_s, ring_r, gr_s, gr_r, spread_s, spread_r, wz_s, wz_r, wx_s, wx_r, wy_s, wy_r, wc_s, wc_r,
-    fc_s, fc_r, fx_s, fx_r, fz_s, fz_r, az_s, az_r, ax_s, ax_r, ac_s, ac_r,
-    sx_s, sx_r, sz_s, sz_r, sa_s, sa_r,
+    sent, ring_r, gr_r, spread, wz_r, wx_r, wy_r, wc_r,
+    fc_r, fx_r, fz_r, az_r, ax_r, ac_r, sx_r, sz_r, sa_r,
 ):
     dp = lax.axis_index("dp")
     y = lax.axis_index("tensor")
@@ -90,9 +89,12 @@
 
     sends = []
 
-    def send(src, dst, ssem, rsem, peer):
+    def arrived(ref, rsem):
+        pltpu.make_async_copy(ref, ref, rsem).wait()
+
+    def send(src, dst, rsem, peer):
         cp = pltpu.make_async_remote_copy(
-            src_ref=src, dst_ref=dst, send_sem=ssem, recv_sem=rsem,
+            src_ref=src, dst_ref=dst, send_sem=sent, recv_sem=rsem,
             device_id=peer, device_id_type=MESH,
         )
         cp.start()
@@ -112,60 +114,61 @@
         for i, (src, dst) in enumerate([
             (acts_hbm, acts_all.at[y]), (weight_hbm, weight), (grads_hbm, grads),
             (basis_hbm, basis),
-        ] + [
-            (fb_hbm.at[0, pl.ds(t * WIDTH, WIDTH)], fb.at[t]) for t in range(NT)
+            (fb_hbm.at[0], fb),
         ])
     ]
     for cp in loads:
         cp.start()
-    loads[0].wait()
-    loads[1].wait()
-    pl.semaphore_wait(barrier, 21 + jnp.where(swaps, 1, 0))
-
-    bh, bc = (dp % NT) // NC, c
-    mine = wbuf.at[group, bh, bc]
-    swap = pltpu.make_async_remote_copy(
-        src_ref=weight, dst_ref=wbuf.at[y, bh, bc], send_sem=spread_s, recv_sem=spread_r,
-        device_id=(pair_dp, group), device_id_type=MESH,
-    )
-
-    @pl.when(swaps)
-    def _():
-        swap.start()
-
-    @pl.when(jnp.logical_not(swaps))
-    def _():
-        wbuf[group, bh, bc] = weight[...]
-
-    right = (dp, (y + 1) % NT)
-    left = (dp, (y + NT - 1) % NT)
-    quarter = TOK // 4
-
-    def block_of(k, way):
-        return (y - k + NT) % NT if way == 0 else (y + k) % NT
-
-    def ring(way, k, h, peer):
-        part = acts_all.at[block_of(k, way), pl.ds(h * quarter, quarter)]
-        return send(part, part, ring_s.at[way, k, h], ring_r.at[way, k, h], peer)
-
-    hops = {}
-    for h in range(4):
-        hops[0, 0, h] = ring(0, 0, h, right)
-        hops[1, 0, h] = ring(1, 0, h, left)
-
     loads[2].wait()
     loads[3].wait()
     grads_all[y] = grads[...]
     bs = pieces(basis[...], 3)
     hs = pieces(folded(mm(bs, grads[...], NTD), 3), 3)
-
-    core_cp, x_cp = {}, {}
+    loads[4].wait()
+    for t in range(NT):
+        fp[t] = folded(mm(bs, fb[t * WIDTH : (t + 1) * WIDTH], NTD), 3)
+    loads[0].wait()
+    loads[1].wait()
+    pl.semaphore_wait(barrier, 21 + jnp.where(swaps, 1, 0))
+
+    bh, bc = (dp % NT) // NC, c
+    mine = wbuf.at[group, bh, bc]
+    swap = pltpu.make_async_remote_copy(
+        src_ref=weight, dst_ref=wbuf.at[y, bh, bc], send_sem=spread.at[0], recv_sem=spread.at[1],
+        device_id=(pair_dp, group), device_id_type=MESH,
+    )
+
+    @pl.when(swaps)
+    def _():
+        swap.start()
+
+    @pl.when(jnp.logical_not(swaps))
+    def _():
+        wbuf[group, bh, bc] = weight[...]
+
+    right = (dp, (y + 1) % NT)
+    left = (dp, (y + NT - 1) % NT)
+    quarter = TOK // 4
+
+    def block_of(k, way):
+        return (y - k + NT) % NT if way == 0 else (y + k) % NT
+
+    def ring(way, k, h, peer):
+        part = acts_all.at[block_of(k, way), pl.ds(h * quarter, quarter)]
+        return send(part, part, ring_r.at[way, k, h], peer)
+
+    hops = {}
+    for h in range(4):
+        hops[0, 0, h] = ring(0, 0, h, right)
+        hops[1, 0, h] = ring(1, 0, h, left)
+
+    core_cp = {}
 
     def add_acts(k, way):
         t = block_of(k, way)
         fp[t] = fp[t] + folded(mm(hs, acts_all[t], NN), 3)
         core_cp[k, way] = send(
-            fp.at[t, pl.ds(32 * (1 - c), 32)], rc.at[t], fc_s.at[t], fc_r.at[t], partner
+            fp.at[t, pl.ds(32 * (1 - c), 32)], rc.at[t], fc_r.at[t], partner
         )
 
     def x_stage(k, way):
@@ -174,18 +177,17 @@
         f1[t] = fp[t, pl.ds(pl.multiple_of(32 * c, 32), 32)] + rc[t]
         for d in range(1, NX):
             to = (x + d) % NX
-            x_cp[k, way, d] = send(
-                f1.at[t, pl.ds(pl.multiple_of(8 * to, 8), 8)], rx.at[d - 1, t],
-                fx_s.at[d - 1, t], fx_r.at[d - 1, t], x_peers[d - 1],
+            send(
+                f1.at[t, pl.ds(pl.multiple_of(8 * to, 8), 8)], rx.at[t, d - 1],
+                fx_r.at[t], x_peers[d - 1],
             )
 
     own = pl.ds(pl.multiple_of(8 * x, 8), 8)
 
     def z_stage(k, way):
         t = block_of(k, way)
-        for d in range(1, NX):
-            x_cp[k, way, d].wait_recv()
-        f2[t] = f1[t, own] + rx[0, t] + rx[1, t] + rx[2, t]
+        arrived(rx.at[t], fx_r.at[t])
+        f2[t] = f1[t, own] + rx[t, 0] + rx[t, 1] + rx[t, 2]
         away = (t - z + NZ) % NZ
 
         @pl.when(away != 0)
@@ -194,8 +196,8 @@
 
     def z_copy(t, away):
         return pltpu.make_async_remote_copy(
-            src_ref=f2.at[t], dst_ref=rz.at[away - 1], send_sem=fz_s.at[away - 1],
-            recv_sem=fz_r.at[away - 1], device_id=(at(x, t, c), y), device_id_type=MESH,
+            src_ref=f2.at[t], dst_ref=rz.at[away - 1], send_sem=sent,
+            recv_sem=fz_r, device_id=(at(x, t, c), y), device_id_type=MESH,
         )
 
     ways = {0: [0], 1: [0, 1], 2: [0, 1], 3: [0, 1], 4: [0]}
@@ -207,70 +209,55 @@
                         hops[way, k - 1, h].wait_recv()
                         if k < 3 or (k == 3 and h // 2 == way):
                             hops[way, k, h] = ring(way, k, h, peer)
-        if k == 0:
-            continue
-        if k == 1:
-            for cp in loads[4:]:
-                cp.wait()
-            for t in range(NT):
-                fp[t] = folded(mm(bs, fb[t], NTD), 3)
-            add_acts(0, 0)
+        if k >= 1:
+            for way in ways[k - 1]:
+                x_stage(k - 1, way)
         for way in ways[k]:
             add_acts(k, way)
         if k == 2:
             @pl.when(swaps)
             def _():
-                swap.wait()
-            wz = [
-                send(mine, mine, wz_s.at[i], wz_r.at[i], z_peers[i]) for i in range(NZ - 1)
-            ]
-        if k >= 1:
-            for way in ways[k - 1]:
-                x_stage(k - 1, way)
+                swap.wait_recv()
+            for i in range(NZ - 1):
+                send(mine, mine, wz_r, z_peers[i])
         if k >= 3:
             for way in ways[k - 3]:
                 z_stage(k - 3, way)
 
-    gcp = [
-        send(grads, grads_all.at[y], gr_s.at[i], gr_r.at[i], y_peers[i])
-        for i in range(NT - 1)
-    ]
+    for i in range(NT - 1):
+        send(grads, grads_all.at[y], gr_r, y_peers[i])
     x_stage(4, 0)
+    for t in range(NT):
+        t0[t] = mm(acts_all[t], grads[...], TN) + fb[t * WIDTH : (t + 1) * WIDTH].astype(F32)
     for k in (2, 3):
         for way in ways[k]:
             z_stage(k, way)
-    for t in range(NT):
-        t0[t] = mm(acts_all[t], grads[...], TN) + fb[t].astype(F32)
     z_stage(4, 0)
-    for cp in wz:
-        cp.wait_recv()
-    wmine = wbuf.at[pl.ds(2 * x, 2), :, c]
-    wx = {
-        way: send(wmine, wmine, wx_s.at[way], wx_r.at[way], x_peers[(0, NX - 2)[way]])
-        for way in (0, 1)
-    }
+    arrived(wbuf.at[0:NZ - 1, 0, 0], wz_r)
+    piece = wbuf.at[pl.ds(2 * x, 2), :, c]
+    wx = [
+        send(piece, piece, wx_r.at[way], x_peers[(0, NX - 2)[way]]) for way in (0, 1)
+    ]
     f3 = f2[z]
     zsum = [z_copy((z + i) % NZ, i) for i in range(1, NZ)]
+    arrived(rz, fz_r)
     for i in range(NZ - 1):
-        zsum[i].wait_recv()
         f3 = f3 + rz[i]
 
     top = f3.astype(BF16).astype(F32)
     f_all[z, q] = jnp.concatenate([top, f3 - top], axis=0).astype(BF16)
     az = [
-        send(f_all.at[z, q], f_all.at[z, q], az_s.at[i], az_r.at[i], z_peers[i])
+        send(f_all.at[z, q], f_all.at[z, q], az_r.at[i], z_peers[i])
         for i in range(NZ - 1)
     ]
-    ax, ac = {}, {}
+    ac = {}
     order = [0, 1, 7, 2, 6, 3, 5, 4]
     for o in order:
         zb = (z - o + NZ) % NZ
         if o:
             az[o - 1].wait_recv()
         for i in range(NX - 1):
-            ax[o, i] = send(
-                f_all.at[zb, q], f_all.at[zb, q], ax_s.at[i, zb], ax_r.at[i, zb], x_peers[i]
-            )
+            send(f_all.at[zb, q], f_all.at[zb, q], ax_r.at[zb], x_peers[i])
 
     def unpaired(pairs):
         v = pairs.reshape(RANK // 8, 2, 8, pairs.shape[1])
@@ -280,10 +267,9 @@
     direct = jnp.zeros((2 * RANK, WIDTH), F32)
     for o in order:
         zb = (z - o + NZ) % NZ
-        for i in range(NX - 1):
-            ax[o, i].wait_recv()
+        arrived(f_all.at[zb, pl.ds(0, NX - 1)], ax_r.at[zb])
         part = f_all.at[zb, pl.ds(NX * c, NX)]
-        ac[o] = send(part, part, ac_s.at[zb], ac_r.at[zb], partner)
+        ac[o] = send(part, part, ac_r.at[zb], partner)
     for some in (order[:4], order[4:]):
         for o in some:
             ac[o].wait_recv()
@@ -291,21 +277,18 @@
             zb = (z - o + NZ) % NZ
             block = f_all[zb].reshape(2 * RANK, WIDTH)
             through = through + mm(block, acts_all[zb], NTD)
-            direct = direct + mm(block, fb[zb], NN)
+            direct = direct + mm(block, fb[pl.ds(pl.multiple_of(zb * WIDTH, WIDTH), WIDTH)], NN)
     local = unpaired(direct) + folded(mm(pieces(unpaired(through), 3), grads[...], NN), 3)
     sp[...] = local.reshape(RANK // 8, 8, WIDTH)
-    sx = []
     for o in range(1, NX * NC):
         to = ((c + o // NX) % NC) * NX + (x + o % NX) % NX
-        sx.append(
-            send(sp.at[to], rs.at[o - 1], sx_s.at[o - 1], sx_r.at[o - 1], xc_peers[o - 1])
-        )
-
-    wy = {}
+        send(sp.at[to], rs.at[o - 1], sx_r, xc_peers[o - 1])
+
+    wy = []
     for way in (0, 1):
         wx[way].wait_recv()
-        part = wbuf.at[2 * ((x + (3, 1)[way]) % NX) + way, :, c]
-        wy[way] = send(part, part, wy_s.at[way], wy_r.at[way], x_peers[(0, NX - 2)[way]])
+        piece = wbuf.at[2 * ((x + (NX - 1, 1)[way]) % NX) + way, :, c]
+        wy.append(send(piece, piece, wy_r.at[way], x_peers[(0, NX - 2)[way]]))
     gram = jnp.zeros((2 * RANK, 2 * RANK), F32)
     for t in range(NT):
         block = f_all[t].reshape(2 * RANK, WIDTH)
@@ -321,29 +304,25 @@
     a = jnp.concatenate([gram, eye], axis=1)
     a = eliminate(a, 0, 12)
 
+    arrived(rs, sx_r)
     s1 = sp[q]
     for i in range(NX * NC - 1):
-        sx[i].wait_recv()
         s1 = s1 + rs[i]
     rsz[z] = s1
-    sz = [
-        send(rsz.at[z], rsz.at[z], sz_s.at[i], sz_r.at[i], z_peers[i]) for i in range(NZ - 1)
-    ]
+    for i in range(NZ - 1):
+        send(rsz.at[z], rsz.at[z], sz_r, z_peers[i])
     a = eliminate(a, 12, 44)
-    for cp in sz:
+    arrived(rsz.at[pl.ds(0, NZ - 1)], sz_r)
+    for cp in wy:
         cp.wait_recv()
-    for way in (0, 1):
-        wy[way].wait_recv()
     whalf = wbuf.at[:, :, c]
-    wc = send(whalf, whalf, wc_s, wc_r, partner)
+    wc = send(whalf, whalf, wc_r, partner)
     s2 = rsz[0]
     for i in range(1, NZ):
         s2 = s2 + rsz[i]
     sfull[q] = s2
-    sa = [
-        send(sfull.at[q], sfull.at[q], sa_s.at[i], sa_r.at[i], xc_peers[i])
-        for i in range(NX * NC - 1)
-    ]
+    for i in range(NX * NC - 1):
+        send(sfull.at[q], sfull.at[q], sa_r, xc_peers[i])
     a = eliminate(a, 44, RANK)
     for t in range(NT):
         ft[t] = (
@@ -351,16 +330,14 @@
         )
     pivots = jnp.sum(a[:, :RANK] * eye, axis=1, keepdims=True)
     inverse = a[:, RANK:]
-    for cp in gcp:
-        cp.wait_recv()
+    arrived(grads_all.at[pl.ds(0, NT - 1)], gr_r)
     wc.wait_recv()
     out = jnp.zeros((TOK, WIDTH), F32)
     for j in range(NT):
         out = out + mm(grads_all[j], wbuf[j].reshape(WIDTH, WIDTH), NTD)
     ig_out[...] = out.astype(BF16)
 
-    for cp in sa:
-        cp.wait_recv()
+    arrived(sfull.at[pl.ds(0, NX * NC - 1)], sa_r)
 
     solved = mm32(inverse, sfull[...].reshape(RANK, WIDTH), NN) / (pivots * 64.0)
     coef = mm32(inverse, solved, TN)
@@ -376,6 +353,10 @@
         cp.wait_send()
     for cp in zsum:
         cp.wait_send()
+
+    @pl.when(swaps)
+    def _():
+        swap.wait_send()
 
 
 def finish(t0, ft, coefs, ig, ig_out, nf_out, up_out, nf, up, sems):
@@ -407,14 +388,14 @@
         pltpu.VMEM((TOK, WIDTH), BF16),
         pltpu.VMEM((ROWS, WIDTH), BF16),
         pltpu.VMEM((RANK, WIDTH), F32),
-        pltpu.VMEM((NT, WIDTH, WIDTH), BF16),
+        pltpu.VMEM((D, WIDTH), BF16),
         pltpu.VMEM((NT, TOK, WIDTH), BF16),
         pltpu.VMEM((NT, TOK, WIDTH), BF16),
         pltpu.VMEM((NT, 4, NC, ROWS, WIDTH), BF16),
         pltpu.VMEM((NT, RANK, WIDTH), F32),
         pltpu.VMEM((NT, RANK // 2, WIDTH), F32),
         pltpu.VMEM((NT, RANK // 2, WIDTH), F32),
-        pltpu.VMEM((NX - 1, NT, 8, WIDTH), F32),
+        pltpu.VMEM((NT, NX - 1, 8, WIDTH), F32),
         pltpu.VMEM((NT, 8, WIDTH), F32),
         pltpu.VMEM((NZ - 1, 8, WIDTH), F32),
         pltpu.VMEM((NT, NX * NC, 16, WIDTH), BF16),
@@ -422,23 +403,24 @@
         pltpu.VMEM((NX * NC - 1, 8, WIDTH), F32),
         pltpu.VMEM((NZ, 8, WIDTH), F32),
         pltpu.VMEM((NX * NC, 8, WIDTH), F32),
-        dma((4 + NT,)),
-        dma((2, 4, 4)), dma((2, 4, 4)),
-        dma((NT - 1,)), dma((NT - 1,)),
-        dma, dma,
-        dma((NZ - 1,)), dma((NZ - 1,)),
-        dma((2,)), dma((2,)),
-        dma((2,)), dma((2,)),
-        dma, dma,
-        dma((NT,)), dma((NT,)),
-        dma((NX - 1, NT)), dma((NX - 1, NT)),
-        dma((NZ - 1,)), dma((NZ - 1,)),
-        dma((NZ - 1,)), dma((NZ - 1,)),
-        dma((NX - 1, NZ)), dma((NX - 1, NZ)),
-        dma((NZ,)), dma((NZ,)),
-        dma((NX * NC - 1,)), dma((NX * NC - 1,)),
-        dma((NZ - 1,)), dma((NZ - 1,)),
-        dma((NX * NC - 1,)), dma((NX * NC - 1,)),
+        dma((5,)),
+        dma,
+        dma((2, 4, 4)),
+        dma,
+        dma((2,)),
+        dma,
+        dma((2,)),
+        dma((2,)),
+        dma,
+        dma((NT,)),
+        dma((NT,)),
+        dma,
+        dma((NZ - 1,)),
+        dma((NZ,)),
+        dma((NZ,)),
+        dma,
+        dma,
+        dma,
     ]
     parts = pl.pallas_call(
         kernel,

time: 74.9 us -> 74.9 us (level); the launches traced: 74.8 us -> 73.7 us
  Pallas kernels: 74.1 us -> 73 us
    pallas_call x1, Pallas kernels: 71.9 us -> 70.8 us  [local(): pl.pallas_call(kernel, out_shape=(jax.ShapeDtypeStruct((TOK, WIDTH), BF16...]
where the time goes in v3:
time: 74.9 us; the launch traced here: 73.7 us
  Pallas kernels  73 us (97%)
    pallas_call x1, Pallas kernels, local(): pl.pallas_call(kernel, out_shape=(jax.ShapeDtypeStruct((TOK, WIDTH), BF16...  70.8 us
    pallas_call x1, Pallas kernels, local(): pl.pallas_call(finish, out_shape=(jax.ShapeDtypeStruct((TOK, WIDTH), BF16...  2.22 us

profile of v3, /device:TPU:1, one launch (start us, length us, event | category | flops | bytes accessed | tf_op | source)
XLA Modules:
  0.0 73.7 jit_solution(12534497596832108067)
XLA Ops:
  0.6 70.8 %shard_map.76 = (bf16[128,384]{1,0:T(8,128)(2,1)S(1)}, f32[8,384,384]{2,1,0:T(8,128)S(1)}, bf16[8,384,128]{2,1,0:T(8,128)(2,1)S(1)}, bf16[2,128,384]{2,1,0:T(8,128)(2,1)S(1)}) custom-call(bf16[128,384]{1,0:T(8,128)(2,1)} %acts_hbm.1, bf16[128,384]{1,0:T(8,128)(2,1)} %grads_hbm.1, bf16[48,384]{1,0:T(8,128)(2,1)} %weight_hbm.1, f32[64,384]{1,0:T(8,128)} %basis_hbm.1, ...), custom_call_target="tpu_custom_call" | custom-call | tf_op jit(solution)/shard_map/pallas_call | solution.py:425
  71.5 2.2 %shard_map.77 = (bf16[128,384]{1,0:T(8,128)(2,1)}, bf16[1,3072,384]{2,1,0:T(8,128)(2,1)}, f32[48,384]{1,0:T(8,128)}) custom-call(f32[8,384,384]{2,1,0:T(8,128)S(1)} %get-tuple-element.7.t0, bf16[8,384,128]{2,1,0:T(8,128)(2,1)S(1)} %get-tuple-element.8.ft, bf16[2,128,384]{2,1,0:T(8,128)(2,1)S(1)} %get-tuple-element.9.coefs, ...), custom_call_target="tpu_custom_call" | custom-call | tf_op jit(solution)/shard_map/pallas_call | solution.py:444

commit v4 on v3

--- a/solution.py
+++ b/solution.py
@@ -60,11 +60,11 @@
 def kernel(
     acts_hbm, grads_hbm, weight_hbm, basis_hbm, fb_hbm,
     ig_out, t0, ft, coefs,
-    grads, weight, basis, fb, acts_all, grads_all, wbuf, fp, rc, f1, rx, f2, rz, f_all,
+    grads, weight, basis, fb, acts_all, grads_all, wbuf, fp, rc, f1, rx, f2, rz, rzx, f_all,
     sp, rs, rsz, sfull,
     in_sem,
     sent, ring_r, gr_r, spread, wz_r, wx_r, wy_r, wc_r,
-    fc_r, fx_r, fz_r, az_r, ax_r, ac_r, sx_r, sz_r, sa_r,
+    fc_r, fx_r, fz_r, zx_r, az_r, ax_r, ac_r, sx_r, sz_r, sa_r,
 ):
     dp = lax.axis_index("dp")
     y = lax.axis_index("tensor")
@@ -184,24 +184,106 @@
 
     own = pl.ds(pl.multiple_of(8 * x, 8), 8)
 
-    def z_stage(k, way):
-        t = block_of(k, way)
-        arrived(rx.at[t], fx_r.at[t])
-        f2[t] = f1[t, own] + rx[t, 0] + rx[t, 1] + rx[t, 2]
-        away = (t - z + NZ) % NZ
-
-        @pl.when(away != 0)
-        def _():
-            z_copy(t, away).start()
-
     def z_copy(t, away):
         return pltpu.make_async_remote_copy(
             src_ref=f2.at[t], dst_ref=rz.at[away - 1], send_sem=sent,
             recv_sem=fz_r, device_id=(at(x, t, c), y), device_id_type=MESH,
         )
 
+    def back_copy(t, i):
+        return pltpu.make_async_remote_copy(
+            src_ref=f_all.at[t, q], dst_ref=f_all.at[t, q], send_sem=sent,
+            recv_sem=az_r.at[t], device_id=z_peers[i], device_id_type=MESH,
+        )
+
+    def x_sum(t):
+        arrived(rx.at[t], fx_r.at[t])
+        return f1[t, own] + rx[t, 0] + rx[t, 1] + rx[t, 2]
+
+    def z_stage(k, way):
+        t = block_of(k, way)
+        f2[t] = x_sum(t)
+        away = (t - z + NZ) % NZ
+
+        @pl.when(away != 0)
+        def _():
+            z_copy(t, away).start()
+
+    def keep(t, f3):
+        top = f3.astype(BF16).astype(F32)
+        f_all[t, q] = jnp.concatenate([top, f3 - top], axis=0).astype(BF16)
+
+    def owner_stage(k, way):
+        t = block_of(k, way)
+
+        @pl.when(t == z)
+        def _():
+            arrived(rz, fz_r)
+            f3 = f2[t]
+            for i in range(NZ - 1):
+                f3 = f3 + rz[i]
+            keep(t, f3)
+            for i in range(NZ - 1):
+                back_copy(t, i).start()
+
+    def back_x_sends(t):
+        for i in range(NX - 1):
+            send(f_all.at[t, q], f_all.at[t, q], ax_r.at[t], x_peers[i])
+
+    def back_x(k, way):
+        t = block_of(k, way)
+
+        @pl.when(t != z)
+        def _():
+            arrived(f_all.at[t, q], az_r.at[t])
+
+        back_x_sends(t)
+
+    def last_z_stage():
+        rzx[z] = x_sum(block_of(4, 0))
+        for i in range(NZ - 1):
+            send(rzx.at[z], rzx.at[z], zx_r, z_peers[i])
+
+    def last_back_x():
+        arrived(rzx.at[pl.ds(0, NZ - 1)], zx_r)
+        f3 = rzx[0]
+        for i in range(1, NZ):
+            f3 = f3 + rzx[i]
+        keep(block_of(4, 0), f3)
+        back_x_sends(block_of(4, 0))
+
+    back_core = {}
+
+    def back_core_stage(k, way):
+        t = block_of(k, way)
+        arrived(f_all.at[t, pl.ds(0, NX - 1)], ax_r.at[t])
+        part = f_all.at[t, pl.ds(NX * c, NX)]
+        back_core[k, way] = send(part, part, ac_r.at[t], partner)
+
+    through = jnp.zeros((2 * RANK, TOK), F32)
+    direct = jnp.zeros((2 * RANK, WIDTH), F32)
+
+    def second_part(through, direct, which):
+        for key in which:
+            back_core[key].wait_recv()
+        for key in which:
+            t = block_of(*key)
+            block = f_all[t].reshape(2 * RANK, WIDTH)
+            rows = pl.ds(pl.multiple_of(t * WIDTH, WIDTH), WIDTH)
+            through = through + mm(block, acts_all[t], NTD)
+            direct = direct + mm(block, fb[rows], NN)
+        return through, direct
+
     ways = {0: [0], 1: [0, 1], 2: [0, 1], 3: [0, 1], 4: [0]}
+
+    def each(stage, k):
+        for way in ways[k]:
+            stage(k, way)
+
     for k in range(5):
+        if k == 4:
+            each(x_stage, 3)
+            each(z_stage, 1)
         if k:
             for h in range(4):
                 for way, peer in ((0, right), (1, left)):
@@ -209,75 +291,53 @@
                         hops[way, k - 1, h].wait_recv()
                         if k < 3 or (k == 3 and h // 2 == way):
                             hops[way, k, h] = ring(way, k, h, peer)
-        if k >= 1:
-            for way in ways[k - 1]:
-                x_stage(k - 1, way)
-        for way in ways[k]:
-            add_acts(k, way)
+        each(add_acts, k)
+        if 1 <= k < 4:
+            each(x_stage, k - 1)
         if k == 2:
             @pl.when(swaps)
             def _():
                 swap.wait_recv()
             for i in range(NZ - 1):
                 send(mine, mine, wz_r, z_peers[i])
-        if k >= 3:
-            for way in ways[k - 3]:
-                z_stage(k - 3, way)
-
+        if k == 3:
+            each(z_stage, 0)
+
+    each(x_stage, 4)
     for i in range(NT - 1):
         send(grads, grads_all.at[y], gr_r, y_peers[i])
-    x_stage(4, 0)
+    each(owner_stage, 0)
+    each(z_stage, 2)
     for t in range(NT):
         t0[t] = mm(acts_all[t], grads[...], TN) + fb[t * WIDTH : (t + 1) * WIDTH].astype(F32)
-    for k in (2, 3):
-        for way in ways[k]:
-            z_stage(k, way)
-    z_stage(4, 0)
     arrived(wbuf.at[0:NZ - 1, 0, 0], wz_r)
     piece = wbuf.at[pl.ds(2 * x, 2), :, c]
     wx = [
         send(piece, piece, wx_r.at[way], x_peers[(0, NX - 2)[way]]) for way in (0, 1)
     ]
-    f3 = f2[z]
-    zsum = [z_copy((z + i) % NZ, i) for i in range(1, NZ)]
-    arrived(rz, fz_r)
-    for i in range(NZ - 1):
-        f3 = f3 + rz[i]
-
-    top = f3.astype(BF16).astype(F32)
-    f_all[z, q] = jnp.concatenate([top, f3 - top], axis=0).astype(BF16)
-    az = [
-        send(f_all.at[z, q], f_all.at[z, q], az_r.at[i], z_peers[i])
-        for i in range(NZ - 1)
-    ]
-    ac = {}
-    order = [0, 1, 7, 2, 6, 3, 5, 4]
-    for o in order:
-        zb = (z - o + NZ) % NZ
-        if o:
-            az[o - 1].wait_recv()
-        for i in range(NX - 1):
-            send(f_all.at[zb, q], f_all.at[zb, q], ax_r.at[zb], x_peers[i])
+    each(z_stage, 3)
+    last_z_stage()
+    each(owner_stage, 1)
+    each(back_x, 0)
+    each(owner_stage, 2)
+    each(owner_stage, 3)
+    each(back_x, 1)
+    last_back_x()
+    each(back_x, 2)
+    each(back_core_stage, 0)
+    each(back_core_stage, 1)
+    each(back_x, 3)
+    each(back_core_stage, 2)
+    through, direct = second_part(through, direct, [(0, 0), (1, 0), (1, 1)])
+    each(back_core_stage, 4)
+    each(back_core_stage, 3)
+    through, direct = second_part(through, direct, [(2, 0), (2, 1)])
+    through, direct = second_part(through, direct, [(4, 0), (3, 0), (3, 1)])
 
     def unpaired(pairs):
         v = pairs.reshape(RANK // 8, 2, 8, pairs.shape[1])
         return (v[:, 0] + v[:, 1]).reshape(RANK, pairs.shape[1])
 
-    through = jnp.zeros((2 * RANK, TOK), F32)
-    direct = jnp.zeros((2 * RANK, WIDTH), F32)
-    for o in order:
-        zb = (z - o + NZ) % NZ
-        arrived(f_all.at[zb, pl.ds(0, NX - 1)], ax_r.at[zb])
-        part = f_all.at[zb, pl.ds(NX * c, NX)]
-        ac[o] = send(part, part, ac_r.at[zb], partner)
-    for some in (order[:4], order[4:]):
-        for o in some:
-            ac[o].wait_recv()
-        for o in some:
-            zb = (z - o + NZ) % NZ
-            block = f_all[zb].reshape(2 * RANK, WIDTH)
-            through = through + mm(block, acts_all[zb], NTD)
-            direct = direct + mm(block, fb[pl.ds(pl.multiple_of(zb * WIDTH, WIDTH), WIDTH)], NN)
     local = unpaired(direct) + folded(mm(pieces(unpaired(through), 3), grads[...], NN), 3)
     sp[...] = local.reshape(RANK // 8, 8, WIDTH)
     for o in range(1, NX * NC):
@@ -351,8 +411,15 @@
 
     for cp in sends:
         cp.wait_send()
-    for cp in zsum:
-        cp.wait_send()
+    for t in [block_of(k, way) for k in range(4) for way in ways[k]]:
+        @pl.when(t != z)
+        def _():
+            z_copy(t, (t - z + NZ) % NZ).wait_send()
+
+        @pl.when(t == z)
+        def _():
+            for i in range(NZ - 1):
+                back_copy(t, i).wait_send()
 
     @pl.when(swaps)
     def _():
@@ -398,6 +465,7 @@
         pltpu.VMEM((NT, NX - 1, 8, WIDTH), F32),
         pltpu.VMEM((NT, 8, WIDTH), F32),
         pltpu.VMEM((NZ - 1, 8, WIDTH), F32),
+        pltpu.VMEM((NZ, 8, WIDTH), F32),
         pltpu.VMEM((NT, NX * NC, 16, WIDTH), BF16),
         pltpu.VMEM((NX * NC, 8, WIDTH), F32),
         pltpu.VMEM((NX * NC - 1, 8, WIDTH), F32),
@@ -415,7 +483,8 @@
         dma((NT,)),
         dma((NT,)),
         dma,
-        dma((NZ - 1,)),
+        dma,
+        dma((NZ,)),
         dma((NZ,)),
         dma((NZ,)),
         dma,

time: 74.9 us -> 72.6 us (0.969); the launches traced: 73.7 us -> 72.4 us
  Pallas kernels: 73 us -> 71.8 us
    pallas_call x1, Pallas kernels: 70.8 us -> 69.6 us  [local(): pl.pallas_call(kernel, out_shape=(jax.ShapeDtypeStruct((TOK, WIDTH), BF16...]
where the time goes in v4:
time: 72.6 us; the launch traced here: 72.4 us
  Pallas kernels  71.8 us (99%)
    pallas_call x1, Pallas kernels, local(): pl.pallas_call(kernel, out_shape=(jax.ShapeDtypeStruct((TOK, WIDTH), BF16...  69.6 us
    pallas_call x1, Pallas kernels, local(): pl.pallas_call(finish, out_shape=(jax.ShapeDtypeStruct((TOK, WIDTH), BF16...  2.22 us

profile of v4, /device:TPU:1, one launch (start us, length us, event | category | flops | bytes accessed | tf_op | source)
XLA Modules:
  0.0 72.4 jit_solution(17248648150444417389)
XLA Ops:
  0.6 69.6 %shard_map.76 = (bf16[128,384]{1,0:T(8,128)(2,1)S(1)}, f32[8,384,384]{2,1,0:T(8,128)S(1)}, bf16[8,384,128]{2,1,0:T(8,128)(2,1)S(1)}, bf16[2,128,384]{2,1,0:T(8,128)(2,1)S(1)}) custom-call(bf16[128,384]{1,0:T(8,128)(2,1)} %acts_hbm.1, bf16[128,384]{1,0:T(8,128)(2,1)} %grads_hbm.1, bf16[48,384]{1,0:T(8,128)(2,1)} %weight_hbm.1, f32[64,384]{1,0:T(8,128)} %basis_hbm.1, ...), custom_call_target="tpu_custom_call" | custom-call | tf_op jit(solution)/shard_map/pallas_call | solution.py:494
  70.2 2.2 %shard_map.77 = (bf16[128,384]{1,0:T(8,128)(2,1)}, bf16[1,3072,384]{2,1,0:T(8,128)(2,1)}, f32[48,384]{1,0:T(8,128)}) custom-call(f32[8,384,384]{2,1,0:T(8,128)S(1)} %get-tuple-element.7.t0, bf16[8,384,128]{2,1,0:T(8,128)(2,1)S(1)} %get-tuple-element.8.ft, bf16[2,128,384]{2,1,0:T(8,128)(2,1)S(1)} %get-tuple-element.9.coefs, ...), custom_call_target="tpu_custom_call" | custom-call | tf_op jit(solution)/shard_map/pallas_call | solution.py:513

commit v5 on v4

--- a/solution.py
+++ b/solution.py
@@ -61,7 +61,7 @@
     acts_hbm, grads_hbm, weight_hbm, basis_hbm, fb_hbm,
     ig_out, t0, ft, coefs,
     grads, weight, basis, fb, acts_all, grads_all, wbuf, fp, rc, f1, rx, f2, rz, rzx, f_all,
-    sp, rs, rsz, sfull,
+    sp, rs, rsz, sfull, through, direct, work, steps,
     in_sem,
     sent, ring_r, gr_r, spread, wz_r, wx_r, wy_r, wc_r,
     fc_r, fx_r, fz_r, zx_r, az_r, ax_r, ac_r, sx_r, sz_r, sa_r,
@@ -77,7 +77,7 @@
 
     q = c * NX + x
     group = dp // NT
-    pair_dp = y * NT + dp % NT
+    pair = (y * NT + dp % NT, group)
     y_peers = [(dp, (y + k) % NT) for k in range(1, NT)]
     z_peers = [(at(x, (z + k) % NZ, c), y) for k in range(1, NZ)]
     xc_peers = [
@@ -101,13 +101,18 @@
         sends.append(cp)
         return cp
 
+    def fence():
+        @pl.when(dp >= 0)
+        def _():
+            steps[0] = 1
+
     barrier = pltpu.get_barrier_semaphore()
-    for peer in y_peers + z_peers + xc_peers:
+    for peer in [y_peers[0], y_peers[NT - 2]] + z_peers + xc_peers:
         pl.semaphore_signal(barrier, inc=1, device_id=peer, device_id_type=MESH)
 
     @pl.when(swaps)
     def _():
-        pl.semaphore_signal(barrier, inc=1, device_id=(pair_dp, group), device_id_type=MESH)
+        pl.semaphore_signal(barrier, inc=1, device_id=pair, device_id_type=MESH)
 
     loads = [
         pltpu.make_async_copy(src, dst, in_sem.at[i])
@@ -119,49 +124,53 @@
     ]
     for cp in loads:
         cp.start()
+    fence()
+    loads[0].wait()
+    loads[1].wait()
+    fence()
+    pl.semaphore_wait(barrier, 16 + jnp.where(swaps, 1, 0))
+
+    fence()
+    mine = wbuf.at[group, z % 4, c]
+    swap = pltpu.make_async_remote_copy(
+        src_ref=weight, dst_ref=wbuf.at[y, z % 4, c], send_sem=spread.at[0], recv_sem=spread.at[1],
+        device_id=pair, device_id_type=MESH,
+    )
+
+    @pl.when(swaps)
+    def _():
+        swap.start()
+
+    @pl.when(jnp.logical_not(swaps))
+    def _():
+        wbuf[y, z % 4, c] = weight[...]
+
+    right = (dp, (y + 1) % NT)
+    left = (dp, (y + NT - 1) % NT)
+    quarter = TOK // 4
+
+    def block_of(k, way):
+        return (y - k + NT) % NT if way == 0 else (y + k) % NT
+
+    def ring(way, k, h, peer):
+        part = acts_all.at[block_of(k, way), pl.ds(h * quarter, quarter)]
+        return send(part, part, ring_r.at[way, k, h], peer)
+
+    hops = {}
+    for h in range(4):
+        hops[0, 0, h] = ring(0, 0, h, right)
+        hops[1, 0, h] = ring(1, 0, h, left)
+
+    fence()
     loads[2].wait()
     loads[3].wait()
     grads_all[y] = grads[...]
     bs = pieces(basis[...], 3)
     hs = pieces(folded(mm(bs, grads[...], NTD), 3), 3)
+    fence()
     loads[4].wait()
     for t in range(NT):
         fp[t] = folded(mm(bs, fb[t * WIDTH : (t + 1) * WIDTH], NTD), 3)
-    loads[0].wait()
-    loads[1].wait()
-    pl.semaphore_wait(barrier, 21 + jnp.where(swaps, 1, 0))
-
-    bh, bc = (dp % NT) // NC, c
-    mine = wbuf.at[group, bh, bc]
-    swap = pltpu.make_async_remote_copy(
-        src_ref=weight, dst_ref=wbuf.at[y, bh, bc], send_sem=spread.at[0], recv_sem=spread.at[1],
-        device_id=(pair_dp, group), device_id_type=MESH,
-    )
-
-    @pl.when(swaps)
-    def _():
-        swap.start()
-
-    @pl.when(jnp.logical_not(swaps))
-    def _():
-        wbuf[group, bh, bc] = weight[...]
-
-    right = (dp, (y + 1) % NT)
-    left = (dp, (y + NT - 1) % NT)
-    quarter = TOK // 4
-
-    def block_of(k, way):
-        return (y - k + NT) % NT if way == 0 else (y + k) % NT
-
-    def ring(way, k, h, peer):
-        part = acts_all.at[block_of(k, way), pl.ds(h * quarter, quarter)]
-        return send(part, part, ring_r.at[way, k, h], peer)
-
-    hops = {}
-    for h in range(4):
-        hops[0, 0, h] = ring(0, 0, h, right)
-        hops[1, 0, h] = ring(1, 0, h, left)
-
     core_cp = {}
 
     def add_acts(k, way):
@@ -260,19 +269,20 @@
         part = f_all.at[t, pl.ds(NX * c, NX)]
         back_core[k, way] = send(part, part, ac_r.at[t], partner)
 
-    through = jnp.zeros((2 * RANK, TOK), F32)
-    direct = jnp.zeros((2 * RANK, WIDTH), F32)
-
-    def second_part(through, direct, which):
+    through[...] = jnp.zeros((2 * RANK, TOK), F32)
+    direct[...] = jnp.zeros((2 * RANK, WIDTH), F32)
+
+    def second_part(which):
         for key in which:
             back_core[key].wait_recv()
+        acts_part, own_part = through[...], direct[...]
         for key in which:
             t = block_of(*key)
             block = f_all[t].reshape(2 * RANK, WIDTH)
             rows = pl.ds(pl.multiple_of(t * WIDTH, WIDTH), WIDTH)
-            through = through + mm(block, acts_all[t], NTD)
-            direct = direct + mm(block, fb[rows], NN)
-        return through, direct
+            acts_part = acts_part + mm(block, acts_all[t], NTD)
+            own_part = own_part + mm(block, fb[rows], NN)
+        through[...], direct[...] = acts_part, own_part
 
     ways = {0: [0], 1: [0, 1], 2: [0, 1], 3: [0, 1], 4: [0]}
 
@@ -282,8 +292,10 @@
 
     for k in range(5):
         if k == 4:
+            fence()
             each(x_stage, 3)
             each(z_stage, 1)
+        fence()
         if k:
             for h in range(4):
                 for way, peer in ((0, right), (1, left)):
@@ -291,64 +303,92 @@
                         hops[way, k - 1, h].wait_recv()
                         if k < 3 or (k == 3 and h // 2 == way):
                             hops[way, k, h] = ring(way, k, h, peer)
+        fence()
         each(add_acts, k)
+        fence()
         if 1 <= k < 4:
             each(x_stage, k - 1)
+        fence()
         if k == 2:
             @pl.when(swaps)
             def _():
                 swap.wait_recv()
             for i in range(NZ - 1):
                 send(mine, mine, wz_r, z_peers[i])
+        fence()
         if k == 3:
             each(z_stage, 0)
 
+    fence()
     each(x_stage, 4)
     for i in range(NT - 1):
         send(grads, grads_all.at[y], gr_r, y_peers[i])
+    fence()
     each(owner_stage, 0)
+    fence()
     each(z_stage, 2)
-    for t in range(NT):
-        t0[t] = mm(acts_all[t], grads[...], TN) + fb[t * WIDTH : (t + 1) * WIDTH].astype(F32)
+    fence()
+    each(z_stage, 3)
+    fence()
     arrived(wbuf.at[0:NZ - 1, 0, 0], wz_r)
     piece = wbuf.at[pl.ds(2 * x, 2), :, c]
     wx = [
         send(piece, piece, wx_r.at[way], x_peers[(0, NX - 2)[way]]) for way in (0, 1)
     ]
-    each(z_stage, 3)
+    fence()
     last_z_stage()
+    fence()
+    for t in range(NT):
+        t0[t] = mm(acts_all[t], grads[...], TN) + fb[t * WIDTH : (t + 1) * WIDTH].astype(F32)
+    fence()
     each(owner_stage, 1)
+    fence()
     each(back_x, 0)
+    fence()
     each(owner_stage, 2)
+    fence()
     each(owner_stage, 3)
+    fence()
     each(back_x, 1)
+    fence()
     last_back_x()
+    fence()
     each(back_x, 2)
+    fence()
     each(back_core_stage, 0)
     each(back_core_stage, 1)
+    fence()
     each(back_x, 3)
+    fence()
     each(back_core_stage, 2)
-    through, direct = second_part(through, direct, [(0, 0), (1, 0), (1, 1)])
+    fence()
+    second_part([(0, 0), (1, 0), (1, 1)])
+    fence()
     each(back_core_stage, 4)
     each(back_core_stage, 3)
-    through, direct = second_part(through, direct, [(2, 0), (2, 1)])
-    through, direct = second_part(through, direct, [(4, 0), (3, 0), (3, 1)])
+    fence()
+    second_part([(2, 0), (2, 1)])
+    fence()
+    second_part([(4, 0), (3, 0), (3, 1)])
 
     def unpaired(pairs):
         v = pairs.reshape(RANK // 8, 2, 8, pairs.shape[1])
         return (v[:, 0] + v[:, 1]).reshape(RANK, pairs.shape[1])
 
-    local = unpaired(direct) + folded(mm(pieces(unpaired(through), 3), grads[...], NN), 3)
+    fence()
+    local = unpaired(direct[...]) + folded(mm(pieces(unpaired(through[...]), 3), grads[...], NN), 3)
     sp[...] = local.reshape(RANK // 8, 8, WIDTH)
     for o in range(1, NX * NC):
         to = ((c + o // NX) % NC) * NX + (x + o % NX) % NX
         send(sp.at[to], rs.at[o - 1], sx_r, xc_peers[o - 1])
 
+    fence()
     wy = []
     for way in (0, 1):
         wx[way].wait_recv()
         piece = wbuf.at[2 * ((x + (NX - 1, 1)[way]) % NX) + way, :, c]
         wy.append(send(piece, piece, wy_r.at[way], x_peers[(0, NX - 2)[way]]))
+    fence()
     gram = jnp.zeros((2 * RANK, 2 * RANK), F32)
     for t in range(NT):
         block = f_all[t].reshape(2 * RANK, WIDTH)
@@ -361,9 +401,11 @@
         lax.broadcasted_iota(jnp.int32, (RANK, RANK), 0)
         == lax.broadcasted_iota(jnp.int32, (RANK, RANK), 1), 1.0, 0.0,
     )
-    a = jnp.concatenate([gram, eye], axis=1)
-    a = eliminate(a, 0, 12)
-
+    work[...] = jnp.concatenate([gram, eye], axis=1)
+    fence()
+    work[...] = eliminate(work[...], 0, 12)
+
+    fence()
     arrived(rs, sx_r)
     s1 = sp[q]
     for i in range(NX * NC - 1):
@@ -371,34 +413,43 @@
     rsz[z] = s1
     for i in range(NZ - 1):
         send(rsz.at[z], rsz.at[z], sz_r, z_peers[i])
-    a = eliminate(a, 12, 44)
+    fence()
+    work[...] = eliminate(work[...], 12, 44)
+    fence()
     arrived(rsz.at[pl.ds(0, NZ - 1)], sz_r)
+    fence()
     for cp in wy:
         cp.wait_recv()
     whalf = wbuf.at[:, :, c]
     wc = send(whalf, whalf, wc_r, partner)
+    fence()
     s2 = rsz[0]
     for i in range(1, NZ):
         s2 = s2 + rsz[i]
     sfull[q] = s2
     for i in range(NX * NC - 1):
         send(sfull.at[q], sfull.at[q], sa_r, xc_peers[i])
-    a = eliminate(a, 44, RANK)
+    fence()
+    work[...] = eliminate(work[...], 44, RANK)
+    fence()
     for t in range(NT):
-        ft[t] = (
-            f_all[t].reshape(2 * RANK, WIDTH).astype(F32).T.astype(BF16)
-        )
-    pivots = jnp.sum(a[:, :RANK] * eye, axis=1, keepdims=True)
-    inverse = a[:, RANK:]
+        columns = f_all[t].reshape(2 * RANK, WIDTH).astype(F32).T.astype(BF16)
+        ft[t] = jnp.concatenate([columns, columns], axis=1)
+    fence()
     arrived(grads_all.at[pl.ds(0, NT - 1)], gr_r)
     wc.wait_recv()
+    fence()
     out = jnp.zeros((TOK, WIDTH), F32)
     for j in range(NT):
         out = out + mm(grads_all[j], wbuf[j].reshape(WIDTH, WIDTH), NTD)
     ig_out[...] = out.astype(BF16)
 
+    fence()
     arrived(sfull.at[pl.ds(0, NX * NC - 1)], sa_r)
 
+    fence()
+    pivots = jnp.sum(work[:, :RANK] * eye, axis=1, keepdims=True)
+    inverse = work[:, RANK:]
     solved = mm32(inverse, sfull[...].reshape(RANK, WIDTH), NN) / (pivots * 64.0)
     coef = mm32(inverse, solved, TN)
     ctop = coef.astype(BF16).astype(F32)
@@ -407,8 +458,9 @@
         v = v.reshape(RANK // 8, 1, 8, WIDTH)
         return jnp.concatenate([v, v], axis=1).reshape(2 * RANK, WIDTH).astype(BF16)
 
-    coefs[0], coefs[1] = doubled(ctop), doubled(coef - ctop)
-
+    coefs[...] = jnp.concatenate([doubled(ctop), doubled(coef - ctop)], axis=0)
+
+    fence()
     for cp in sends:
         cp.wait_send()
     for t in [block_of(k, way) for k in range(4) for way in ways[k]]:
@@ -428,7 +480,7 @@
 
 def finish(t0, ft, coefs, ig, ig_out, nf_out, up_out, nf, up, sems):
     def low_rank(left_side):
-        return mm(left_side, coefs[0], NN) + mm(left_side, coefs[1], NN)
+        return mm(left_side, coefs[...], NN)
 
     stores = [pltpu.make_async_copy(ig, ig_out, sems.at[NT])]
     stores[0].start()
@@ -471,6 +523,10 @@
         pltpu.VMEM((NX * NC - 1, 8, WIDTH), F32),
         pltpu.VMEM((NZ, 8, WIDTH), F32),
         pltpu.VMEM((NX * NC, 8, WIDTH), F32),
+        pltpu.VMEM((2 * RANK, TOK), F32),
+        pltpu.VMEM((2 * RANK, WIDTH), F32),
+        pltpu.VMEM((RANK, 2 * RANK), F32),
+        pltpu.SMEM((1,), jnp.int32),
         dma((5,)),
         dma,
         dma((2, 4, 4)),
@@ -496,8 +552,8 @@
         out_shape=(
             jax.ShapeDtypeStruct((TOK, WIDTH), BF16),
             jax.ShapeDtypeStruct((NT, WIDTH, WIDTH), F32),
-            jax.ShapeDtypeStruct((NT, WIDTH, 2 * RANK), BF16),
-            jax.ShapeDtypeStruct((2, 2 * RANK, WIDTH), BF16),
+            jax.ShapeDtypeStruct((NT, WIDTH, 4 * RANK), BF16),
+            jax.ShapeDtypeStruct((4 * RANK, WIDTH), BF16),
         ),
         in_specs=[hbm] * 5,
         out_specs=(vmem,) * 4,

time: 72.6 us -> 69.2 us (0.953)
  Pallas kernels: 71.8 us -> 68 us
    pallas_call x1, Pallas kernels: 69.6 us -> 66.1 us  [local(): pl.pallas_call(kernel, out_shape=(jax.ShapeDtypeStruct((TOK, WIDTH), BF16...]
where the time goes in v5:
time: 69.2 us; the launch traced here: 68.6 us
  Pallas kernels  68 us (98%)
    pallas_call x1, Pallas kernels, local(): pl.pallas_call(kernel, out_shape=(jax.ShapeDtypeStruct((TOK, WIDTH), BF16...  66.1 us
    pallas_call x1, Pallas kernels, local(): pl.pallas_call(finish, out_shape=(jax.ShapeDtypeStruct((TOK, WIDTH), BF16...  1.81 us

profile of v5, /device:TPU:1, one launch (start us, length us, event | category | flops | bytes accessed | tf_op | source)
XLA Modules:
  0.0 68.6 jit_solution(11740189037032945630)
XLA Ops:
  0.6 66.1 %shard_map.76 = (bf16[128,384]{1,0:T(8,128)(2,1)S(1)}, f32[8,384,384]{2,1,0:T(8,128)S(1)}, bf16[8,384,256]{2,1,0:T(8,128)(2,1)S(1)}, bf16[256,384]{1,0:T(8,128)(2,1)S(1)}) custom-call(bf16[128,384]{1,0:T(8,128)(2,1)} %acts_hbm.1, bf16[128,384]{1,0:T(8,128)(2,1)} %grads_hbm.1, bf16[48,384]{1,0:T(8,128)(2,1)} %weight_hbm.1, f32[64,384]{1,0:T(8,128)} %basis_hbm.1, ...), custom_call_target="tpu_custom_call" | custom-call | tf_op jit(solution)/shard_map/pallas_call | solution.py:550
  66.8 1.8 %shard_map.77 = (bf16[128,384]{1,0:T(8,128)(2,1)}, bf16[1,3072,384]{2,1,0:T(8,128)(2,1)}, f32[48,384]{1,0:T(8,128)}) custom-call(f32[8,384,384]{2,1,0:T(8,128)S(1)} %get-tuple-element.7.t0, bf16[8,384,256]{2,1,0:T(8,128)(2,1)S(1)} %get-tuple-element.8.ft, bf16[256,384]{1,0:T(8,128)(2,1)S(1)} %get-tuple-element.9.coefs, bf16[128,384]{1,0:T(8,128)(2,1)S(1)} %get-tuple-element.10.ig), custom_call_target="tpu_custom_call" | custom-call | tf_op jit(solution)/shard_map/pallas_call | solution.py:569
